TPU v7x, 128 devices: a whole 4x4x4 slice. The times are simulated.
128 devices in a mesh: section: 2 (over z_hi), shard: 2 (over core), replica: 32 (over x, y, z_lo).
Axes of the slice: x: 4, y: 4, z: 4 (z_hi: 2, z_lo: 2; z = z_hi * 2 + z_lo), core: 2. Of those that a mesh axis runs over, the one named last changes fastest.
Arguments:
- tokens: bfloat16 [2, 8192, 576], P(None, ('shard', 'replica')), may hold values from -6 to 6
- cotangent: bfloat16 [2, 8192, 576], P(None, ('shard', 'replica')), may hold values from -6 to 6
- seq_lengths: int32 [2, 128], P(None, ('shard', 'replica')), may hold values from 0 to 128, as said below
- gain_attn: bfloat16 [2, 576], P('section', 'shard'), may hold values from 0.5 to 1.5
- w_query: bfloat16 [2, 576, 576], P('section', 'shard'), may hold values from -0.25 to 0.25
- w_key: bfloat16 [2, 576, 192], P('section', 'shard'), may hold values from -0.25 to 0.25
- w_value: bfloat16 [2, 576, 192], P('section', 'shard'), may hold values from -0.25 to 0.25
- w_out: bfloat16 [2, 576, 576], P('section', 'shard'), may hold values from -1 to 1
- gain_ffn: bfloat16 [2, 576], P('section', 'shard'), may hold values from 0.5 to 1.5
- w_gate: bfloat16 [2, 576, 1536], P('section', 'shard'), may hold values from -0.25 to 0.25
- w_up: bfloat16 [2, 576, 1536], P('section', 'shard'), may hold values from -0.25 to 0.25
- w_down: bfloat16 [2, 1536, 576], P('section', 'shard'), may hold values from -0.21875 to 0.21875
Outputs:
- activations: bfloat16 [2, 2, 8192, 576], P('section', None, ('shard', 'replica'))
- input_grads: bfloat16 [2, 2, 8192, 576], P('section', None, ('shard', 'replica'))
- grad_gain_attn: float32 [2, 576], P('section', 'shard')
- grad_query: float32 [2, 576, 576], P('section', 'shard')
- grad_key: float32 [2, 576, 192], P('section', 'shard')
- grad_value: float32 [2, 576, 192], P('section', 'shard')
- grad_out: float32 [2, 576, 576], P('section', 'shard')
- grad_gain_ffn: float32 [2, 576], P('section', 'shard')
- grad_gate: float32 [2, 576, 1536], P('section', 'shard')
- grad_up: float32 [2, 576, 1536], P('section', 'shard')
- grad_down: float32 [2, 1536, 576], P('section', 'shard')
Inputs may be any that keep to these rules, and one draw needn't show every extreme that they name: `seq_lengths`: the 2 lengths of one token group's micro-batch sum to at most 128; in every micro-batch one token group holds a single sequence of 128.
All inputs are finite; a program needn't handle non-finite values.
Results may differ from a plain program's by a relative error of at most 0.03.
Values may be sent and summed in bfloat16 or wider, within the bound.
A program may use at most 128 MiB of HBM per device.

v0:
```python
import math

import jax
import jax.numpy as jnp
from jax import lax
from jax.sharding import PartitionSpec as P

H = 9
KV = 3
HD = 64


eps_norm = 1e-05
rope_base = 100000.0


def side_by_side(arrays, axis, dim, along):
    widths = [math.prod(a.shape[along:]) for a in arrays]
    both = jnp.concatenate(
        [a.reshape(*a.shape[:along], w) for a, w in zip(arrays, widths)], axis=along
    )
    result = lax.all_gather(both, axis, axis=dim, tiled=True)
    blocks = jnp.split(result, [sum(widths[:k]) for k in range(1, len(widths))], axis=along)
    return tuple(
        (b.reshape(*result.shape[:along], *a.shape[along:]) for a, b in zip(arrays, blocks))
    )


def passed_along(shard, axis, by):
    length = lax.axis_size(axis)
    pairs = [(i, i + by) for i in range(length) if 0 <= i + by < length]
    return lax.ppermute(shard, axis, pairs)


def cut_along(shard, dim, length):
    before, after = (shard.shape[:dim], shard.shape[dim + 1 :])
    return jnp.moveaxis(shard.reshape(*before, length, -1, *after), dim, 0)


def summed_on_arrival(shard, axis, dim):
    length = lax.axis_size(axis)
    blocks = lax.all_to_all(cut_along(shard, dim, length), axis, 0, 0, tiled=True)
    return jnp.sum(blocks.astype(jnp.float32), axis=0)


def as_sent(shard):
    return jax.tree.map(lambda a: a.astype(jnp.bfloat16) if a.dtype == jnp.float32 else a, shard)


def layout(lengths, row_count):
    row_ids = jnp.arange(row_count, dtype=jnp.int32)
    seq_ends = jnp.cumsum(lengths, axis=-1)
    passed = (row_ids[:, None] >= seq_ends[None, :]).astype(jnp.int32)
    segment = jnp.sum(passed, axis=-1)
    starts = jnp.sum(passed * lengths[None, :], axis=-1)
    position = row_ids - starts
    live_rows = (row_ids < seq_ends[-1:]).astype(jnp.float32)
    return (segment, position, live_rows)


def rope_tables(position):
    half_dim = HD // 2
    freq_idx = jnp.arange(half_dim, dtype=jnp.float32)
    inverse = jnp.exp(freq_idx * (-2.0 * math.log(rope_base) / HD))
    angles = position.astype(jnp.float32)[:, None] * inverse[None, :]
    cosine = jnp.cos(angles)
    sine_val = jnp.sin(angles)
    return (jnp.concatenate([cosine, cosine], -1), jnp.concatenate([sine_val, sine_val], -1))


def rotate(values, cosine, sine_val):
    half_dim = values.shape[-1] // 2
    turned = jnp.concatenate([-values[..., half_dim:], values[..., :half_dim]], -1)
    return values * cosine[:, None, :] + turned * sine_val[:, None, :]


def rotate_back(grads, cosine, sine_val):
    half_dim = grads.shape[-1] // 2
    scaled = grads * sine_val[:, None, :]
    back = jnp.concatenate([scaled[..., half_dim:], -scaled[..., :half_dim]], -1)
    return grads * cosine[:, None, :] + back


def norm_back(upper, normed, scale_val):
    return scale_val * (upper - normed * jnp.mean(upper * normed, axis=-1, keepdims=True))


def forward_parts(hidden_in, weights, segment, position):
    gain_one, w_query, w_key, w_value, w_out, gain_two, w_gate, w_up, w_down = weights
    row_count = hidden_in.shape[0]
    scale_one = lax.rsqrt(jnp.mean(hidden_in * hidden_in, axis=-1, keepdims=True) + eps_norm)
    normed = hidden_in * scale_one
    entry = (normed * gain_one.astype(jnp.float32)).astype(jnp.bfloat16)
    query = jnp.dot(entry, w_query, preferred_element_type=jnp.float32).reshape(row_count, H, HD)
    keys_raw = jnp.dot(entry, w_key, preferred_element_type=jnp.float32).reshape(row_count, KV, HD)
    values_b = (
        jnp.dot(entry, w_value, preferred_element_type=jnp.float32)
        .astype(jnp.bfloat16)
        .reshape(row_count, KV, HD)
    )
    cosine, sine_val = rope_tables(position)
    query_rot = (
        rotate(query, cosine, sine_val).astype(jnp.bfloat16).reshape(row_count, KV, H // KV, HD)
    )
    key_rot = rotate(keys_raw, cosine, sine_val).astype(jnp.bfloat16)
    scores = jnp.einsum(
        "rkgd,ckd->kgrc", query_rot, key_rot, preferred_element_type=jnp.float32
    ) * HD ** (-0.5)
    row_ids = jnp.arange(row_count)
    allowed = (segment[:, None] == segment[None, :]) & (row_ids[None, :] <= row_ids[:, None])
    scores = jnp.where(allowed, scores, -1e30)
    probs = jax.nn.softmax(scores, axis=-1)
    probs_b = probs.astype(jnp.bfloat16)
    mixed = jnp.einsum("kgrc,ckd->rkgd", probs_b, values_b, preferred_element_type=jnp.float32)
    mixed = mixed.astype(jnp.bfloat16).reshape(row_count, H * HD)
    middle = hidden_in + jnp.dot(mixed, w_out, preferred_element_type=jnp.float32)
    scale_two = lax.rsqrt(jnp.mean(middle * middle, axis=-1, keepdims=True) + eps_norm)
    normed_two = middle * scale_two
    second = (normed_two * gain_two.astype(jnp.float32)).astype(jnp.bfloat16)
    gate_val = jnp.dot(second, w_gate, preferred_element_type=jnp.float32)
    up_val = jnp.dot(second, w_up, preferred_element_type=jnp.float32)
    sigmoid_val = jax.nn.sigmoid(gate_val)
    inner = (gate_val * sigmoid_val * up_val).astype(jnp.bfloat16)
    return {
        "scale_one": scale_one,
        "normed": normed,
        "entry": entry,
        "query_rot": query_rot,
        "key_rot": key_rot,
        "values_b": values_b,
        "cosine": cosine,
        "sine_val": sine_val,
        "probs": probs,
        "probs_b": probs_b,
        "mixed": mixed,
        "middle": middle,
        "scale_two": scale_two,
        "normed_two": normed_two,
        "second": second,
        "gate_val": gate_val,
        "up_val": up_val,
        "sigmoid_val": sigmoid_val,
        "inner": inner,
    }


def forward_layer(hidden_in, weights, segment, position):
    kept = forward_parts(hidden_in, weights, segment, position)
    return kept["middle"] + jnp.dot(kept["inner"], weights[8], preferred_element_type=jnp.float32)


def backward_layer(hidden_in, upstream, weights, segment, position):
    gain_one, w_query, w_key, w_value, w_out, gain_two, w_gate, w_up, w_down = weights
    kept = forward_parts(hidden_in, weights, segment, position)
    row_count = hidden_in.shape[0]
    down_b = upstream.astype(jnp.bfloat16)
    grad_down = jnp.einsum("rf,rd->fd", kept["inner"], down_b, preferred_element_type=jnp.float32)
    d_inner = jnp.einsum("rd,fd->rf", down_b, w_down, preferred_element_type=jnp.float32)
    gate_val, up_val, sigmoid_val = (kept["gate_val"], kept["up_val"], kept["sigmoid_val"])
    d_gate = (d_inner * up_val * sigmoid_val * (1.0 + gate_val * (1.0 - sigmoid_val))).astype(
        jnp.bfloat16
    )
    d_up = (d_inner * gate_val * sigmoid_val).astype(jnp.bfloat16)
    grad_gate = jnp.einsum("rd,rf->df", kept["second"], d_gate, preferred_element_type=jnp.float32)
    grad_up = jnp.einsum("rd,rf->df", kept["second"], d_up, preferred_element_type=jnp.float32)
    d_second = jnp.einsum("rf,df->rd", d_gate, w_gate, preferred_element_type=jnp.float32)
    d_second = d_second + jnp.einsum("rf,df->rd", d_up, w_up, preferred_element_type=jnp.float32)
    grad_gain_two = jnp.sum(d_second * kept["normed_two"], axis=0)
    d_middle = upstream + norm_back(
        d_second * gain_two.astype(jnp.float32), kept["normed_two"], kept["scale_two"]
    )
    branch_b = d_middle.astype(jnp.bfloat16)
    grad_out = jnp.einsum("re,rd->ed", kept["mixed"], branch_b, preferred_element_type=jnp.float32)
    d_mixed = jnp.einsum("rd,ed->re", branch_b, w_out, preferred_element_type=jnp.float32)
    d_mixed = d_mixed.astype(jnp.bfloat16).reshape(row_count, KV, H // KV, HD)
    d_probs = jnp.einsum(
        "rkgd,ckd->kgrc", d_mixed, kept["values_b"], preferred_element_type=jnp.float32
    )
    d_values = jnp.einsum(
        "kgrc,rkgd->ckd", kept["probs_b"], d_mixed, preferred_element_type=jnp.float32
    )
    d_values = d_values.astype(jnp.bfloat16).reshape(row_count, KV * HD)
    probs = kept["probs"]
    row_total = jnp.sum(d_probs * probs, axis=-1, keepdims=True)
    d_scores = (probs * (d_probs - row_total) * HD ** (-0.5)).astype(jnp.bfloat16)
    d_query = jnp.einsum(
        "kgrc,ckd->rkgd", d_scores, kept["key_rot"], preferred_element_type=jnp.float32
    )
    d_keys = jnp.einsum(
        "kgrc,rkgd->ckd", d_scores, kept["query_rot"], preferred_element_type=jnp.float32
    )
    d_query = rotate_back(d_query.reshape(row_count, H, HD), kept["cosine"], kept["sine_val"])
    d_query = d_query.astype(jnp.bfloat16).reshape(row_count, H * HD)
    d_keys = (
        rotate_back(d_keys, kept["cosine"], kept["sine_val"])
        .astype(jnp.bfloat16)
        .reshape(row_count, KV * HD)
    )
    entry = kept["entry"]
    grad_query = jnp.einsum("rd,re->de", entry, d_query, preferred_element_type=jnp.float32)
    grad_key = jnp.einsum("rd,re->de", entry, d_keys, preferred_element_type=jnp.float32)
    grad_value = jnp.einsum("rd,re->de", entry, d_values, preferred_element_type=jnp.float32)
    d_entry = jnp.einsum("re,de->rd", d_query, w_query, preferred_element_type=jnp.float32)
    d_entry = d_entry + jnp.einsum("re,de->rd", d_keys, w_key, preferred_element_type=jnp.float32)
    d_entry = d_entry + jnp.einsum(
        "re,de->rd", d_values, w_value, preferred_element_type=jnp.float32
    )
    grad_gain_one = jnp.sum(d_entry * kept["normed"], axis=0)
    d_input = d_middle + norm_back(
        d_entry * gain_one.astype(jnp.float32), kept["normed"], kept["scale_one"]
    )
    grads = (
        grad_gain_one,
        grad_query,
        grad_key,
        grad_value,
        grad_out,
        grad_gain_two,
        grad_gate,
        grad_up,
        grad_down,
    )
    return (d_input, grads)


def shards(
    tokens,
    cotangent,
    seq_lengths,
    gain_attn,
    w_query,
    w_key,
    w_value,
    w_out,
    gain_ffn,
    w_gate,
    w_up,
    w_down,
):
    micro = tokens.shape[0]
    row_count = tokens.shape[1]
    width = tokens.shape[2]
    first = lax.axis_index("section") == 0
    gathered = (
        *side_by_side(
            (gain_attn, w_query, w_key, w_value, w_out, gain_ffn, w_gate, w_up), "shard", 1, 2
        ),
        lax.all_gather(w_down, "shard", axis=1, tiled=True),
    )
    weights = tuple((piece[0] for piece in gathered))
    layouts = [layout(seq_lengths[index], row_count) for index in range(micro)]

    def pick(early, late):
        seg_a, pos_a, live_a = layouts[early]
        seg_b, pos_b, live_b = layouts[late]
        return (jnp.where(first, seg_a, seg_b), jnp.where(first, pos_a, pos_b))

    received = jnp.zeros((row_count, width), jnp.bfloat16)
    section_inputs = []
    section_outputs = []
    for tick in range(micro + 1):
        own_rows = tokens[min(tick, micro - 1)]
        layer_in = jnp.where(first, own_rows, received)
        segment, position = pick(min(tick, micro - 1), max(tick - 1, 0))
        result = forward_layer(layer_in.astype(jnp.float32), weights, segment, position).astype(
            jnp.bfloat16
        )
        section_inputs.append(layer_in)
        section_outputs.append(result)
        if tick < micro:
            received = passed_along(result, "section", 1)
    activations = jnp.stack(
        [
            jnp.where(first, section_outputs[index], section_outputs[index + 1])
            for index in range(micro)
        ]
    )
    inputs_by_mb = [
        jnp.where(first, section_inputs[index], section_inputs[index + 1]) for index in range(micro)
    ]
    grad_received = jnp.zeros((row_count, width), jnp.bfloat16)
    grad_ticks = []
    totals = None
    for tick in range(micro + 1):
        early = max(tick - 1, 0)
        late = min(tick, micro - 1)
        layer_in = jnp.where(first, inputs_by_mb[early], inputs_by_mb[late])
        if tick < micro:
            own_cot = cotangent[late].astype(jnp.float32) * layouts[late][2][:, None]
        else:
            own_cot = jnp.zeros((row_count, width), jnp.float32)
        upstream = jnp.where(first, grad_received.astype(jnp.float32), own_cot)
        segment, position = pick(early, late)
        d_input, grads = backward_layer(
            layer_in.astype(jnp.float32), upstream, weights, segment, position
        )
        d_input_b = d_input.astype(jnp.bfloat16)
        grad_ticks.append(d_input_b)
        totals = grads if totals is None else tuple((a + b for a, b in zip(totals, grads)))
        if tick < micro:
            grad_received = passed_along(d_input_b, "section", -1)
    input_grads = jnp.stack(
        [jnp.where(first, grad_ticks[index + 1], grad_ticks[index]) for index in range(micro)]
    )
    full_grads = tuple((g[None] for g in totals))
    grouped = jax.tree.map(lambda part: summed_on_arrival(part, "shard", 1), as_sent(full_grads))
    owned = jax.tree.map(
        lambda part: part.astype(jnp.float32), lax.psum(as_sent(grouped), "replica")
    )
    return (
        activations[None],
        input_grads[None],
        owned[0],
        owned[1],
        owned[2],
        owned[3],
        owned[4],
        owned[5],
        owned[6],
        owned[7],
        owned[8],
    )


def solution(mesh):
    in_specs = (
        P(None, ("shard", "replica"), None),
        P(None, ("shard", "replica"), None),
        P(None, ("shard", "replica")),
        P("section", "shard"),
        P("section", "shard", None),
        P("section", "shard", None),
        P("section", "shard", None),
        P("section", "shard", None),
        P("section", "shard"),
        P("section", "shard", None),
        P("section", "shard", None),
        P("section", "shard", None),
    )
    out_specs = (
        P("section", None, ("shard", "replica"), None),
        P("section", None, ("shard", "replica"), None),
        P("section", "shard"),
        P("section", "shard", None),
        P("section", "shard", None),
        P("section", "shard", None),
        P("section", "shard", None),
        P("section", "shard"),
        P("section", "shard", None),
        P("section", "shard", None),
        P("section", "shard", None),
    )
    return jax.shard_map(shards, mesh=mesh, in_specs=in_specs, out_specs=out_specs, check_vma=False)
```

profile of v0, /device:TPU:0, one launch (start us, length us, event | category | flops | bytes accessed | tf_op | source)
XLA Modules:
  0.0 627.5 jit_solution(9803920860311983403)
XLA Ops:
  8.9 6.1 concatenate.91
  22.1 13.8 %all-gather.3.cloned.1.call-done = bf16[1,576,4610]{2,1,0:T(8,128)(2,1)} async-done(((bf16[1,288,4610]{2,1,0:T(8,128)(2,1)}), bf16[1,576,4610]{2,1,0:T(8,128)(2,1)}) %all-gather.3.cloned.1.call-update) | async-done | bytes 5310736 | tf_op jit(solution)/shard_map/all_gather | solution.py:22
  45.8 2.6 fusion.224
  48.3 3.3 all-gather.5.cloned.1.call-done
  51.7 3.7 fusion.77
  55.4 5.6 collective-permute-start
  69.9 2.6 fusion.225
  72.5 3.7 fusion.74
  76.2 6.4 %collective-permute-start.1 = (bf16[128,576]{0,1:T(8,128)(2,1)S(1)}, bf16[128,576]{0,1:T(8,128)(2,1)S(1)}, u32[]{:S(2)}, u32[]{:S(2)}) collective-permute-start(bf16[128,576]{0,1:T(8,128)(2,1)S(1)} %fusion.74), channel_id=1, source_target_pairs={{0,64},{1,65},{2,66},{3,67},{4,68},{5,69},{6,70},{7,71},{8,72},{9,... | collective-permute-start | bytes 442376 | tf_op jit(solution)/shard_map/ppermute | solution.py:32
  87.6 2.1 multiply_reduce_fusion.11
  96.5 2.2 multiply_reduce_fusion.7
  99.4 2.8 fusion.311
  102.3 2.5 fusion.314
  111.4 2.6 fusion.89
  114.1 2.6 broadcast_multiply_fusion.2
  132.9 2.4 fusion.456
  135.3 2.4 fusion.458
  137.7 2.4 fusion.140
  140.4 2.1 fusion.451
  145.4 2.2 multiply_reduce_fusion.9
  151.9 2.4 fusion.309
  165.1 2.4 fusion.94
  167.5 2.3 broadcast_multiply_fusion
  171.8 2.5 fusion.317
  174.4 3.5 fusion.457
  177.9 2.4 fusion.459
  187.5 2.5 fusion.141
  197.7 2.4 broadcast_multiply_fusion.1
  204.6 2.1 fusion.60
  210.4 4.1 all-to-all-start.2
  214.6 2.2 fusion.61
  223.9 4.4 add_convert_fusion
  228.3 4.1 transpose_reshape.29
  233.9 3.4 add_convert_fusion.3
  244.9 3.4 all-to-all-start.3
  250.1 3.5 all-to-all-start.1
  255.5 3.5 all-to-all-start.4
  260.9 4.7 all-to-all-start.6
  268.4 3.9 all-to-all-start.7
  272.3 2.9 reduce_sum.508
  275.2 4.7 all-to-all-start.8
  282.6 2.9 reduce_sum.512
  291.3 2.6 fusion.226
  293.9 3.8 fusion.83
  304.2 3.7 all_to_all.45
  308.9 3.7 all_to_all.46
  312.7 82.1 %all-reduce = (bf16[1,288]{1,0:T(2,128)(2,1)S(1)}, bf16[1,288]{1,0:T(2,128)(2,1)S(1)}) all-reduce(bf16[1,288]{1,0:T(2,128)(2,1)S(1)} %reduce_sum.494, bf16[1,288]{1,0:T(2,128)(2,1)S(1)} %reduce_sum.507), channel_id=1, replica_groups=mesh['section'=2,'shard'=2,'replica'=32] {'replica'}, use_global_device_ids=true, to_apply=%region_43.44 | all-reduce | flops 576 | bytes 2304 | tf_op jit(solution)/shard_map/psum | solution.py:308
  396.8 212.3 %all-reduce.4.cloned.1.call-done = (bf16[1,288,192]{1,2,0:T(8,128)(2,1)}, bf16[1,288,192]{1,2,0:T(8,128)(2,1)}, bf16[1,288,576]{2,1,0:T(8,128)(2,1)}, bf16[1,288...) async-done(((bf16[1,288,192]{1,2,0:T(8,128)(2,1)}, bf16[1,288,192]{1,2,0:T(8,128)(2,1)}, ...) | async-done | bytes 3538960 | tf_op jit(solution)/shard_map/psum | solution.py:308
  (531 shorter events, 158.4 us)
Async XLA Ops:
  7.2 28.7 %all-gather.3.cloned.1.call-start = ((), (), s32[]{:S(2)}) async-start(), calls=%async_computation.9 | async-start | bytes 8183808 | tf_op jit(solution)/shard_map/all_gather | solution.py:22
  15.0 36.6 %all-gather.5.cloned.1.call-start = ((), (), s32[]{:S(2)}) async-start(), calls=%async_computation.10 | async-start | bytes 2654208 | tf_op jit(solution)/shard_map/all_gather | solution.py:248
  17.0 70.0 %copy-start.104 = (pred[128,128]{0,1:T(8,128)(4,1)}, pred[128,128]{0,1:T(8,128)(4,1)S(1)}, u32[]{:S(2)}) copy-start(pred[128,128]{0,1:T(8,128)(4,1)S(1)} %fusion.326) | copy-start | bytes 49156
  18.7 65.5 %copy-start.34 = (f32[128,64]{0,1:T(8,128)}, f32[128,64]{0,1:T(8,128)S(1)}, u32[]{:S(2)}) copy-start(f32[128,64]{0,1:T(8,128)S(1)} %pad_maximum_fusion.4) | copy-start | bytes 98308
  19.5 72.9 %copy-start.47 = (f32[128,64]{0,1:T(8,128)}, f32[128,64]{0,1:T(8,128)S(1)}, u32[]{:S(2)}) copy-start(f32[128,64]{0,1:T(8,128)S(1)} %pad_maximum_fusion.8) | copy-start | bytes 98308
  19.5 131.3 %copy-start.28 = (f32[128,64]{0,1:T(8,128)}, f32[128,64]{0,1:T(8,128)S(1)}, u32[]{:S(2)}) copy-start(f32[128,64]{0,1:T(8,128)S(1)} %pad_maximum_fusion.7) | copy-start | bytes 98308
  55.3 9.5 %copy-start.94 = (bf16[128,576]{0,1:T(8,128)(2,1)}, bf16[128,576]{0,1:T(8,128)(2,1)S(1)}, u32[]{:S(2)}) copy-start(bf16[128,576]{0,1:T(8,128)(2,1)S(1)} %fusion.77) | copy-start | bytes 442372
  55.4 10.0 %copy-start.105 = (pred[128,128]{0,1:T(8,128)(4,1)S(1)}, pred[128,128]{0,1:T(8,128)(4,1)}, u32[]{:S(2)}) copy-start(pred[128,128]{0,1:T(8,128)(4,1)} %fusion.325) | copy-start | bytes 49156
  55.4 8.8 %collective-permute-start = (bf16[128,576]{0,1:T(8,128)(2,1)S(1)}, bf16[128,576]{0,1:T(8,128)(2,1)S(1)}, u32[]{:S(2)}, u32[]{:S(2)}) collective-permute-start(bf16[128,576]{0,1:T(8,128)(2,1)S(1)} %fusion.77), channel_id=1, source_target_pairs={{0,64},{1,65},{2,66},{3,67},{4,68},{5,69},{6,70},{7,71},{8,72},{9,... | collective-permute-start | bytes 442376 | tf_op jit(solution)/shard_map/ppermute | solution.py:32
  72.5 10.2 %copy-start.95 = (bf16[128,576]{0,1:T(8,128)(2,1)S(1)}, bf16[128,576]{0,1:T(8,128)(2,1)}, u32[]{:S(2)}) copy-start(bf16[128,576]{0,1:T(8,128)(2,1)} %copy-done.94) | copy-start | bytes 442372
  76.2 11.4 %copy-start.87 = (bf16[128,576]{0,1:T(8,128)(2,1)}, bf16[128,576]{0,1:T(8,128)(2,1)S(1)}, u32[]{:S(2)}) copy-start(bf16[128,576]{0,1:T(8,128)(2,1)S(1)} %fusion.74) | copy-start | bytes 442372
  76.2 13.5 %collective-permute-start.1 = (bf16[128,576]{0,1:T(8,128)(2,1)S(1)}, bf16[128,576]{0,1:T(8,128)(2,1)S(1)}, u32[]{:S(2)}, u32[]{:S(2)}) collective-permute-start(bf16[128,576]{0,1:T(8,128)(2,1)S(1)} %fusion.74), channel_id=1, source_target_pairs={{0,64},{1,65},{2,66},{3,67},{4,68},{5,69},{6,70},{7,71},{8,72},{9,... | collective-permute-start | bytes 442376 | tf_op jit(solution)/shard_map/ppermute | solution.py:32
  83.4 44.6 %copy-start.117 = (f32[128]{0:T(128)}, f32[128]{0:T(128)S(1)}, u32[]{:S(2)}) copy-start(f32[128]{0:T(128)S(1)} %add_rsqrt_fusion.5) | copy-start | bytes 1540
  89.7 9.0 %copy-start.39 = (f32[128,576]{0,1:T(8,128)}, f32[128,576]{0,1:T(8,128)S(1)}, u32[]{:S(2)}) copy-start(f32[128,576]{0,1:T(8,128)S(1)} %get-tuple-element.160) | copy-start | bytes 884740
  89.8 9.0 %copy-start.131 = (f32[128]{0:T(128)}, f32[128]{0:T(128)S(1)}, u32[]{:S(2)}) copy-start(f32[128]{0:T(128)S(1)} %add_rsqrt_fusion.4) | copy-start | bytes 1540
  89.9 38.1 %copy-start.5 = (bf16[128,576]{0,1:T(8,128)(2,1)}, bf16[128,576]{0,1:T(8,128)(2,1)S(1)}, u32[]{:S(2)}) copy-start(bf16[128,576]{0,1:T(8,128)(2,1)S(1)} %get-tuple-element.63) | copy-start | bytes 442372
  96.4 8.3 %copy-start.84 = (bf16[3,64,3,128]{3,1,2,0:T(8,128)(2,1)}, bf16[3,64,3,128]{3,1,2,0:T(8,128)(2,1)S(1)}, u32[]{:S(2)}) copy-start(bf16[3,64,3,128]{3,1,2,0:T(8,128)(2,1)S(1)} %convolution_convert_fusion.3) | copy-start | bytes 442372
  98.9 58.1 %copy-start.10 = (bf16[128,576]{0,1:T(8,128)(2,1)}, bf16[128,576]{0,1:T(8,128)(2,1)S(1)}, u32[]{:S(2)}) copy-start(bf16[128,576]{0,1:T(8,128)(2,1)S(1)} %get-tuple-element.121) | copy-start | bytes 442372
  118.2 10.6 %copy-start.78 = (bf16[3,64,128]{2,1,0:T(8,128)(2,1)}, bf16[3,64,128]{2,1,0:T(8,128)(2,1)S(1)}, u32[]{:S(2)}) copy-start(bf16[3,64,128]{2,1,0:T(8,128)(2,1)S(1)} %fusion.86) | copy-start | bytes 147460
  118.2 9.8 %copy-start.22 = (f32[128,576]{0,1:T(8,128)S(1)}, f32[128,576]{0,1:T(8,128)}, u32[]{:S(2)}) copy-start(f32[128,576]{0,1:T(8,128)} %copy-done.21) | copy-start | bytes 884740
  122.0 9.4 %copy-start.98 = (bf16[3,64,3,128]{3,1,2,0:T(8,128)(2,1)S(1)}, bf16[3,64,3,128]{3,1,2,0:T(8,128)(2,1)}, u32[]{:S(2)}) copy-start(bf16[3,64,3,128]{3,1,2,0:T(8,128)(2,1)} %copy-done.97) | copy-start | bytes 442372
  124.6 8.3 %copy-start.72 = (bf16[128,1536]{1,0:T(8,128)(2,1)S(1)}, bf16[128,1536]{1,0:T(8,128)(2,1)}, u32[]{:S(2)}) copy-start(bf16[128,1536]{1,0:T(8,128)(2,1)} %copy-done.71) | copy-start | bytes 1179652
  140.2 10.6 %copy-start.80 = (f32[128,3,32]{0,2,1:T(8,128)}, f32[128,3,32]{0,2,1:T(8,128)S(1)}, u32[]{:S(2)}) copy-start(f32[128,3,32]{0,2,1:T(8,128)S(1)} %get-tuple-element.113) | copy-start | bytes 147460
  140.2 10.6 %copy-start.82 = (f32[128,3,32]{0,2,1:T(8,128)}, f32[128,3,32]{0,2,1:T(8,128)S(1)}, u32[]{:S(2)}) copy-start(f32[128,3,32]{0,2,1:T(8,128)S(1)} %get-tuple-element.114) | copy-start | bytes 147460
  140.3 8.7 %copy-start.16 = (f32[3,64,3,128]{3,1,2,0:T(8,128)S(1)}, f32[3,64,3,128]{3,1,2,0:T(8,128)}, u32[]{:S(2)}) copy-start(f32[3,64,3,128]{3,1,2,0:T(8,128)} %fusion.89) | copy-start | bytes 884740
  140.3 8.7 %copy-start.36 = (f32[128,9,64]{0,2,1:T(8,128)S(1)}, f32[128,9,64]{0,2,1:T(8,128)}, u32[]{:S(2)}) copy-start(f32[128,9,64]{0,2,1:T(8,128)} %get-tuple-element.80) | copy-start | bytes 884740
  140.3 14.0 %slice-start.2 = ((s8[5455872]{0:T(1024)(128)(4,1)}), s8[1261568]{0:T(1024)(128)(4,1)S(1)}, s32[]{:S(2)}) async-start(s8[5455872]{0:T(1024)(128)(4,1)} %bitcast.644), calls=%async_computation.14 | async-start | bytes 2523136
  140.3 8.6 %copy-start.114 = (bf16[128,3,64,1]{0,2,3,1:T(8,128)(2,1)}, bf16[128,3,64,1]{0,2,3,1:T(8,128)(2,1)S(1)}, u32[]{:S(2)}) copy-start(bf16[128,3,64,1]{0,2,3,1:T(8,128)(2,1)S(1)} %fusion.328) | copy-start | bytes 147460
  140.3 8.6 %copy-start.118 = (f32[128]{0:T(128)S(1)}, f32[128]{0:T(128)}, u32[]{:S(2)}) copy-start(f32[128]{0:T(128)} %copy-done.117) | copy-start | bytes 1540
  140.4 10.2 %copy-start.92 = (bf16[128,9,64]{0,2,1:T(8,128)(2,1)}, bf16[128,9,64]{0,2,1:T(8,128)(2,1)S(1)}, u32[]{:S(2)}) copy-start(bf16[128,9,64]{0,2,1:T(8,128)(2,1)S(1)} %fusion.194) | copy-start | bytes 442372
  145.4 9.0 %slice-start.3 = ((s8[5455872]{0:T(1024)(128)(4,1)}), s8[4194304]{0:T(1024)(128)(4,1)S(1)}, s32[]{:S(2)}) async-start(s8[5455872]{0:T(1024)(128)(4,1)} %bitcast.644), calls=%async_computation.15 | async-start | bytes 8388608
  147.6 12.4 %collective-permute-start.2 = (bf16[128,576]{0,1:T(8,128)(2,1)}, bf16[128,576]{0,1:T(8,128)(2,1)S(1)}, u32[]{:S(2)}, u32[]{:S(2)}) collective-permute-start(bf16[128,576]{0,1:T(8,128)(2,1)} %get-tuple-element.100), channel_id=1, source_target_pairs={{64,0},{65,1},{66,2},{67,3},{68,4},{69,5},{70,6},{71,7},{72,8},{73... | collective-permute-start | bytes 442376 | tf_op jit(solution)/shard_map/ppermute | solution.py:32
  169.8 10.7 %slice-start.4 = ((s8[5455872]{0:T(1024)(128)(4,1)}), s8[1261568]{0:T(1024)(128)(4,1)S(1)}, s32[]{:S(2)}) async-start(s8[5455872]{0:T(1024)(128)(4,1)} %bitcast.646), calls=%async_computation.16 | async-start | bytes 2523136
  183.1 9.4 %collective-permute-start.3 = (bf16[128,576]{0,1:T(8,128)(2,1)S(1)}, bf16[128,576]{0,1:T(8,128)(2,1)S(1)}, u32[]{:S(2)}, u32[]{:S(2)}) collective-permute-start(bf16[128,576]{0,1:T(8,128)(2,1)S(1)} %get-tuple-element.61), channel_id=1, source_target_pairs={{64,0},{65,1},{66,2},{67,3},{68,4},{69,5},{70,6},{71,7},{72,8},{73... | collective-permute-start | bytes 442376 | tf_op jit(solution)/shard_map/ppermute | solution.py:32
  202.0 21.9 %copy-start.4 = (f32[1536,576]{0,1:T(8,128)S(1)}, f32[1536,576]{0,1:T(8,128)}, u32[]{:S(2)}) copy-start(f32[1536,576]{0,1:T(8,128)} %fusion.140) | copy-start | bytes 10616836
  210.4 34.5 %all-to-all-start.2 = ((bf16[2,1,288,192]{2,3,1,0:T(8,128)(2,1)}), bf16[2,1,288,192]{2,3,1,0:T(8,128)(2,1)}, u32[]{:S(2)}, u32[]{:S(2)}) async-start(bf16[2,1,288,192]{2,3,1,0:T(8,128)(2,1)} %copy.112), calls=%async_computation.2 | async-start | bytes 589824 | tf_op jit(solution)/shard_map/all_to_all | solution.py:42
  244.9 5.2 all-to-all-start.3
  250.1 5.4 all-to-all-start.1
  255.5 5.4 all-to-all-start.4
  260.9 7.4 %all-to-all-start.6 = ((bf16[2,1,288,1536]{3,2,1,0:T(8,128)(2,1)}), bf16[2,1,288,1536]{3,2,1,0:T(8,128)(2,1)}, u32[]{:S(2)}, u32[]{:S(2)}) async-start(bf16[2,1,288,1536]{3,2,1,0:T(8,128)(2,1)} %bitcast.171), calls=%async_computation.6 | async-start | bytes 3538944 | tf_op jit(solution)/shard_map/all_to_all | solution.py:42
  268.4 6.8 %all-to-all-start.7 = ((bf16[2,1,288,1536]{3,2,1,0:T(8,128)(2,1)}), bf16[2,1,288,1536]{3,2,1,0:T(8,128)(2,1)S(1)}, u32[]{:S(2)}, u32[]{:S(2)}) async-start(bf16[2,1,288,1536]{3,2,1,0:T(8,128)(2,1)} %bitcast.174), calls=%async_computation.7 | async-start | bytes 3538944 | tf_op jit(solution)/shard_map/all_to_all | solution.py:42
  275.2 7.4 %all-to-all-start.8 = ((bf16[2,1,768,576]{2,3,1,0:T(8,128)(2,1)}), bf16[2,1,768,576]{2,3,1,0:T(8,128)(2,1)}, u32[]{:S(2)}, u32[]{:S(2)}) async-start(bf16[2,1,768,576]{2,3,1,0:T(8,128)(2,1)} %copy.120), calls=%async_computation.8 | async-start | bytes 3538944 | tf_op jit(solution)/shard_map/all_to_all | solution.py:42
  279.9 329.2 %all-reduce.4.cloned.1.call-start = ((), (), s32[]{:S(2)}) async-start(), calls=%async_computation.11 | async-start | bytes 7372800 | tf_op jit(solution)/shard_map/psum | solution.py:308
  297.7 10.3 %copy-start.122 = (f32[576]{0:T(1024)S(1)}, f32[576]{0:T(1024)}, u32[]{:S(2)}) copy-start(f32[576]{0:T(1024)} %get-tuple-element.37) | copy-start | bytes 6916
  297.7 10.3 %copy-start.123 = (f32[576]{0:T(1024)S(1)}, f32[576]{0:T(1024)}, u32[]{:S(2)}) copy-start(f32[576]{0:T(1024)} %get-tuple-element.35) | copy-start | bytes 6916
  297.7 98.2 %copy-start.52 = (bf16[128,576]{0,1:T(8,128)(2,1)S(1)}, bf16[128,576]{0,1:T(8,128)(2,1)}, u32[]{:S(2)}) copy-start(bf16[128,576]{0,1:T(8,128)(2,1)} %copy-done.51) | copy-start | bytes 442372
  297.7 98.4 %copy-start.57 = (bf16[1,128,576]{1,2,0:T(8,128)(2,1)S(1)}, bf16[1,128,576]{1,2,0:T(8,128)(2,1)}, u32[]{:S(2)}) copy-start(bf16[1,128,576]{1,2,0:T(8,128)(2,1)} %get-tuple-element.60) | copy-start | bytes 442372
  609.1 8.9 %copy-start.42 = (bf16[1,288,1536]{2,1,0:T(8,128)(2,1)S(1)}, bf16[1,288,1536]{2,1,0:T(8,128)(2,1)}, u32[]{:S(2)}) copy-start(bf16[1,288,1536]{2,1,0:T(8,128)(2,1)} %get-tuple-element.58) | copy-start | bytes 2654212
  (114 other events, 497.3 us)
Sparse Core Ops, SparseCore 0:
  15.1 20.6 all-gather.2
  37.5 14.1 all-gather.4
  285.7 323.3 all-reduce.3
where the time goes:
time: 636 us; the launch traced here: 627 us
  waiting for transfers between devices  239 us (38%)
  matrix products  156 us (25%)
  blocking collectives  89.5 us (14%)
  other arithmetic  47.2 us (7%)
  starting transfers between devices  43 us (7%)
  local copies, waits for them, and re-layouts  36.5 us (6%)
  between operations  16.6 us (3%)
    psum x1, waiting for transfers between devices, shards(): lax.psum(as_sent(grouped), 'replica')  212 us
    psum x1, blocking collectives, shards(): lax.psum(as_sent(grouped), 'replica')  82.1 us
    all_to_all x7, starting transfers between devices, summed_on_arrival(): lax.all_to_all(cut_along(shard, dim, length), axis, 0, 0, tiled=True)  27.9 us
    ppermute x4, starting transfers between devices, passed_along(): return lax.ppermute(shard, axis, pairs)  15 us
    dot_general x6, matrix products, forward_parts(): gate_val = jnp.dot(second, w_gate, preferred_element_type=jnp.float32)  14.7 us
    all_gather x1, waiting for transfers between devices, side_by_side(): result = lax.all_gather(both, axis, axis=dim, tiled=True)  13.8 us
    another operation x6, local copies, waits for them, and re-layouts, cut_along(): return jnp.moveaxis(shard.reshape(*before, length, -1, *after), dim, 0)  12.8 us
  transfers between devices with their start and end apart: 14, of which 9 were waited for; matrix products, arithmetic and copies ran while one was open for 16% of the time, Pallas kernels for 0%

commit v1 on v0

v1 whole, which is shorter than its diff:
```python
import functools
import math

import jax
import jax.numpy as jnp
from jax import lax
from jax.experimental import pallas as pl
from jax.experimental.pallas import tpu as pltpu
from jax.sharding import PartitionSpec as P

MESH = pl.DeviceIdType.MESH
F32 = jnp.float32
BF16 = jnp.bfloat16

D = 576
HD = 64
FF = 1536
ROWS = 128
MICRO = 2
M = MICRO * ROWS
OWN = D // 2
EPS = 1e-05
BASE = 100000.0
VMEM_LIMIT = 56 * 1024 * 1024

GATE = 0
UP = GATE + 12 * OWN
DOWN = UP + 12 * OWN
QKV = DOWN + 6 * D
OUT = QKV + 8 * OWN
GAIN = OUT + 4 * OWN
USED = GAIN + OWN
FLAT = 14336
HALF = FLAT // 2
P1 = HALF // 4
P2 = P1 // 4
P3 = P2 // 2


def dot(a, b):
    return lax.dot_general(a, b, (((1,), (0,)), ((), ())), preferred_element_type=F32)


def dot_nt(a, b):
    return lax.dot_general(a, b, (((1,), (1,)), ((), ())), preferred_element_type=F32)


def dot_tn(a, b):
    return lax.dot_general(a, b, (((0,), (0,)), ((), ())), preferred_element_type=F32)


def lanes():
    return lax.broadcasted_iota(jnp.int32, (ROWS, 128), 1)


def slots():
    return lax.broadcasted_iota(jnp.int32, (ROWS, 128), 0)


def ends(lens, m):
    return lens[m, 0], lens[m, 0] + lens[m, 1]


def segment_of(ids, first_end, last_end):
    return jnp.where(ids >= first_end, 1, 0) + jnp.where(ids >= last_end, 1, 0)


def tables(lens, cs, sn):
    lane = lanes()
    inverse = jnp.exp((lane % 32).astype(F32) * (-2.0 * math.log(BASE) / HD))
    for m in range(MICRO):
        first_end, last_end = ends(lens, m)
        r = slots()
        position = r - jnp.where(r >= first_end, lens[m, 0], 0)
        position = position - jnp.where(r >= last_end, lens[m, 1], 0)
        angle = position.astype(F32) * inverse
        sine = jnp.sin(angle)
        cs[m] = jnp.cos(angle)
        sn[m] = jnp.where(lane % 64 < 32, -sine, sine)


def turned(u, lane):
    return jnp.where(lane % 64 < 32, pltpu.roll(u, 96, 1), pltpu.roll(u, 32, 1))


def both_halves(u, half, lane):
    return jnp.where(lane // 64 == half, u, pltpu.roll(u, 64, 1))


def norm_scale(x):
    return lax.rsqrt(jnp.mean(x * x, axis=-1, keepdims=True) + EPS)


def gains_of(wq):
    turned_gains = wq[:, 896:1024].astype(F32).T
    return turned_gains[64:65], turned_gains[65:66]


def norm_back(upper, normed, scale):
    return scale * (upper - normed * jnp.mean(upper * normed, axis=-1, keepdims=True))


def attention_forward(x, lens, wq, wo, g1, s):
    entry = (x * norm_scale(x) * g1).astype(BF16)
    s["ent"][...] = entry
    qkv = dot(entry, wq[...])
    lane = lanes()
    for m in range(MICRO):
        rows = slice(m * ROWS, (m + 1) * ROWS)
        cosine, sine = s["cs"][m], s["sn"][m]
        first_end, last_end = ends(lens, m)
        allowed = (
            segment_of(slots(), first_end, last_end) == segment_of(lane, first_end, last_end)
        ) & (lane <= slots())
        allowed = jnp.concatenate([allowed.astype(F32)] * 3, axis=0) > 0.5
        blocks = []
        for b in range(6):
            u = qkv[rows, 128 * b : 128 * b + 128]
            blocks.append(u * cosine + turned(u, lane) * sine)
        heads = []
        for kv in range(3):
            i = m * 3 + kv
            kj = 9 + kv
            key = both_halves(blocks[kj // 2], kj % 2, lane).astype(BF16)
            vb = qkv[rows, 768 + 128 * (kv // 2) : 896 + 128 * (kv // 2)]
            value = both_halves(vb, kv % 2, lane).astype(BF16)
            query = jnp.concatenate(
                [
                    jnp.where(lane // 64 == j % 2, blocks[j // 2], 0.0).astype(BF16)
                    for j in range(3 * kv, 3 * kv + 3)
                ],
                axis=0,
            )
            s["kd"][i] = key
            s["vd"][i] = value
            s["qs"][i] = query
            scores = jnp.where(allowed, dot_nt(query, key) * HD**-0.5, -1e30)
            weights = jnp.exp(scores - jnp.max(scores, axis=-1, keepdims=True))
            probs = weights / jnp.sum(weights, axis=-1, keepdims=True)
            s["pr"][i] = probs
            out = dot(probs.astype(BF16), value)
            heads += [out[ROWS * g : ROWS * (g + 1)] for g in range(3)]
        for b in range(4):
            s["mix"][rows, 128 * b : 128 * b + 128] = jnp.where(
                lane < 64, heads[2 * b], heads[2 * b + 1]
            ).astype(BF16)
        s["mix"][rows, 512:576] = heads[8][:, :64].astype(BF16)
    middle = x + dot(s["mix"][...], wo[...])
    s["mid"][...] = middle
    return middle


def feed_forward(middle, g2, wg, wu, wd, s, keep):
    second = (middle * norm_scale(middle) * g2).astype(BF16)
    s["sec"][...] = second
    for j in range(0, FF, 256):
        cols = slice(j, j + 256)
        gate = dot(second, wg[:, cols])
        up = dot(second, wu[:, cols])
        sig = 1.0 / (1.0 + jnp.exp(-gate))
        swish = gate * sig
        s["inn"][:, cols] = (swish * up).astype(BF16)
        if keep:
            s["fa"][:, cols] = up * sig * (1.0 + gate * (1.0 - sig))
            s["fb"][:, cols] = swish
    return middle + dot(s["inn"][...], wd[...])


def backward_inputs(x, dy, wq, wo, g1, g2, wg, wu, wd, s, t):
    middle = s["mid"][...]
    scale_two = norm_scale(middle)
    n2 = middle * scale_two
    df = dy.astype(BF16)
    t["df"][...] = df
    for j in range(0, FF, 256):
        cols = slice(j, j + 256)
        d_inner = dot_nt(df, wd[cols, :])
        t["dg"][:, cols] = (d_inner * s["fa"][:, cols]).astype(BF16)
        t["du"][:, cols] = (d_inner * s["fb"][:, cols]).astype(BF16)
    d_second = dot_nt(t["dg"][...], wg[...]) + dot_nt(t["du"][...], wu[...])
    gain_two = jnp.sum(d_second * n2, axis=0, keepdims=True)
    d_middle = dy + norm_back(d_second * g2, n2, scale_two)
    branch = d_middle.astype(BF16)
    t["db"][...] = branch
    d_mixed = dot_nt(branch, wo[...])
    lane = lanes()
    for m in range(MICRO):
        rows = slice(m * ROWS, (m + 1) * ROWS)
        cosine, sine = s["cs"][m], s["sn"][m]
        dq, dk, dv = [], [], []
        for kv in range(3):
            i = m * 3 + kv
            parts = []
            for j in range(3 * kv, 3 * kv + 3):
                if j < 8:
                    block = d_mixed[rows, 128 * (j // 2) : 128 * (j // 2) + 128]
                    block = jnp.where(lane // 64 == j % 2, block, 0.0)
                else:
                    block = jnp.concatenate(
                        [d_mixed[rows, 512:576], jnp.zeros((ROWS, 64), F32)], axis=1
                    )
                parts.append(block.astype(BF16))
            upper = jnp.concatenate(parts, axis=0)
            probs = s["pr"][i]
            d_probs = dot_nt(upper, s["vd"][i])
            value = dot_tn(probs.astype(BF16), upper)
            dv.append(value + pltpu.roll(value, 64, 1))
            total = jnp.sum(d_probs * probs, axis=-1, keepdims=True)
            d_scores = (probs * (d_probs - total) * HD**-0.5).astype(BF16)
            query = dot(d_scores, s["kd"][i])
            dq += [query[ROWS * g : ROWS * (g + 1)] for g in range(3)]
            key = dot_tn(d_scores, s["qs"][i])
            dk.append(key + pltpu.roll(key, 64, 1))
        heads = dq + dk
        for b in range(6):
            u = jnp.where(lane < 64, heads[2 * b], heads[2 * b + 1])
            t["dqkv"][rows, 128 * b : 128 * b + 128] = (
                u * cosine - turned(u, lane) * sine
            ).astype(BF16)
        t["dqkv"][rows, 768:896] = jnp.where(lane < 64, dv[0], dv[1]).astype(BF16)
        t["dqkv"][rows, 896:1024] = jnp.where(lane < 64, dv[2], 0.0).astype(BF16)
    d_entry = dot_nt(t["dqkv"][...], wq[...])
    scale_one = norm_scale(x)
    n1 = x * scale_one
    gain_one = jnp.sum(d_entry * n1, axis=0, keepdims=True)
    dx = d_middle + norm_back(d_entry * g1, n1, scale_one)
    return dx, d_middle, gain_one, gain_two


def flat_store(flat, start, block, count):
    flat[0, start : start + count] = block[:count].astype(BF16)
    flat[1, start : start + count] = block[count:].astype(BF16)


def weight_grads(d_middle, gain_one, gain_two, s, t, flat):
    second_t = s["sec"][...].T
    for b in range(0, 12, 2):
        for key, start in (("dg", GATE), ("du", UP)):
            g = dot(second_t, t[key][:, 128 * b : 128 * b + 256])
            flat_store(flat, start + b * OWN, g[:, :128], OWN)
            flat_store(flat, start + (b + 1) * OWN, g[:, 128:], OWN)
    df_t = t["df"][...].T
    for b in range(0, 12, 2):
        g = dot(df_t, s["inn"][:, 128 * b : 128 * b + 256]).astype(BF16)
        owner, first = b // 6, DOWN + (b % 6) * D
        flat[owner, first : first + D] = g[:, :128]
        flat[owner, first + D : first + 2 * D] = g[:, 128:]
    entry_t = s["ent"][...].T
    mixed_t = s["mix"][...].T
    for b in range(0, 6, 2):
        g = dot(entry_t, t["dqkv"][:, 128 * b : 128 * b + 256])
        flat_store(flat, QKV + b * OWN, g[:, :128], OWN)
        flat_store(flat, QKV + (b + 1) * OWN, g[:, 128:], OWN)
    g = dot(entry_t, t["dqkv"][:, 768:1024])
    flat_store(flat, QKV + 6 * OWN, g[:, :128], OWN)
    rest = jnp.concatenate([d_middle[:, 512:576], jnp.zeros((M, 64), F32)], axis=1)
    rest = pltpu.roll(rest, 64, 1).astype(BF16)
    flat_store(flat, QKV + 7 * OWN, g[:, 128:] + dot(mixed_t, rest), OWN)
    for b in range(0, 4, 2):
        g = dot(mixed_t, t["db"][:, 128 * b : 128 * b + 256])
        flat_store(flat, OUT + b * OWN, g[:, :128], OWN)
        flat_store(flat, OUT + (b + 1) * OWN, g[:, 128:], OWN)
    row = lax.broadcasted_iota(jnp.int32, (128, D), 0)
    gains = jnp.where(row == 0, gain_one, jnp.where(row == 1, gain_two, 0.0)).T
    flat_store(flat, GAIN, gains, OWN)
    flat[0, USED:] = jnp.zeros((FLAT - USED, 128), BF16)
    flat[1, USED:] = jnp.zeros((FLAT - USED, 128), BF16)


SAVED = {
    "ent": ((M, D), BF16),
    "qs": ((6, 3 * ROWS, 128), BF16),
    "kd": ((6, ROWS, 128), BF16),
    "vd": ((6, ROWS, 128), BF16),
    "pr": ((6, 3 * ROWS, 128), F32),
    "mix": ((M, D), BF16),
    "mid": ((M, D), F32),
    "sec": ((M, D), BF16),
    "inn": ((M, FF), BF16),
    "fa": ((M, FF), F32),
    "fb": ((M, FF), F32),
    "cs": ((MICRO, ROWS, 128), F32),
    "sn": ((MICRO, ROWS, 128), F32),
}
TEMPS = {
    "df": ((M, D), BF16),
    "dg": ((M, FF), BF16),
    "du": ((M, FF), BF16),
    "db": ((M, D), BF16),
    "dqkv": ((M, 1024), BF16),
}


def scratch(table, names=None):
    return [pltpu.VMEM(*table[k]) for k in (names or table)]


def rows_of(ref):
    return jnp.concatenate([ref[0], ref[1]], axis=0).astype(F32)


def store_rows(ref, value):
    for m in range(MICRO):
        ref[m] = value[m * ROWS : (m + 1) * ROWS].astype(BF16)


def forward_kernel(lens, x_ref, wq, wo, wg, wu, wd, y_ref, *saved):
    s = dict(zip(SAVED, saved))
    g1, g2 = gains_of(wq)
    tables(lens, s["cs"], s["sn"])
    middle = attention_forward(rows_of(x_ref), lens, wq, wo, g1, s)
    store_rows(y_ref, feed_forward(middle, g2, wg, wu, wd, s, False))


def middle_kernel(lens, x_ref, cot, wq, wo, wg, wu, wd, y_ref, dx_ref, *refs):
    s = dict(zip(SAVED, refs))
    t = dict(zip(TEMPS, refs[len(SAVED) :]))
    g1, g2 = gains_of(wq)
    tables(lens, s["cs"], s["sn"])
    x = rows_of(x_ref)
    middle = attention_forward(x, lens, wq, wo, g1, s)
    store_rows(y_ref, feed_forward(middle, g2, wg, wu, wd, s, True))
    dy = live_rows(cot, lens)
    dx = backward_inputs(x, dy, wq, wo, g1, g2, wg, wu, wd, s, t)[0]
    store_rows(dx_ref, dx)


def live_rows(cot, lens):
    ids = lax.broadcasted_iota(jnp.int32, (ROWS, D), 0)
    return jnp.concatenate(
        [jnp.where(ids < ends(lens, m)[1], cot[m].astype(F32), 0.0) for m in range(MICRO)], axis=0
    )


def last_kernel(lens, x_ref, cot, received, wq, wo, wg, wu, wd, *refs):
    s = dict(zip(SAVED, refs))
    dx_ref, flat = refs[len(SAVED) : len(SAVED) + 2]
    t = dict(zip(TEMPS, refs[len(SAVED) + 2 :]))
    g1, g2 = gains_of(wq)
    x = rows_of(x_ref)
    first = lax.axis_index("section") == 0
    dy = jnp.where(first, rows_of(received), live_rows(cot, lens))
    dx, d_middle, gain_one, gain_two = backward_inputs(x, dy, wq, wo, g1, g2, wg, wu, wd, s, t)
    store_rows(dx_ref, dx)
    weight_grads(d_middle, gain_one, gain_two, s, t, flat)


def vmem(n):
    return [pl.BlockSpec(memory_space=pltpu.VMEM)] * n


def smem():
    return [pl.BlockSpec(memory_space=pltpu.SMEM)]


def shapes(table):
    return [jax.ShapeDtypeStruct(*v) for v in table.values()]


def params(**kw):
    return pltpu.CompilerParams(vmem_limit_bytes=VMEM_LIMIT, **kw)


ROW_SHAPE = jax.ShapeDtypeStruct((MICRO, ROWS, D), BF16)


def run_forward(lens, x, weights):
    return pl.pallas_call(
        forward_kernel,
        out_shape=ROW_SHAPE,
        in_specs=smem() + vmem(6),
        out_specs=vmem(1)[0],
        scratch_shapes=scratch(SAVED),
        compiler_params=params(),
    )(lens, x, *weights)


def run_middle(lens, x, cot, weights):
    out = pl.pallas_call(
        middle_kernel,
        out_shape=[ROW_SHAPE, ROW_SHAPE] + shapes(SAVED),
        in_specs=smem() + vmem(7),
        out_specs=vmem(2 + len(SAVED)),
        scratch_shapes=scratch(TEMPS),
        compiler_params=params(),
    )(lens, x, cot, *weights)
    return out[0], out[1], out[2:]


def run_last(lens, x, cot, received, weights, saved):
    return pl.pallas_call(
        last_kernel,
        out_shape=[ROW_SHAPE, jax.ShapeDtypeStruct((2, FLAT, 128), BF16)],
        in_specs=smem() + vmem(8 + len(SAVED)),
        out_specs=vmem(2),
        scratch_shapes=scratch(TEMPS),
        compiler_params=params(),
    )(lens, x, cot, received, *weights, *saved)


def gather_kernel(*refs):
    ins, outs = refs[:5], refs[5:10]
    send, recv, local = refs[10:]
    section, core, replica = (lax.axis_index(a) for a in ("section", "shard", "replica"))
    other = (section, 1 - core, replica)
    barrier = pltpu.get_barrier_semaphore()
    pl.semaphore_signal(barrier, inc=1, device_id=other, device_id_type=MESH)
    pl.semaphore_wait(barrier, 1)
    copies = []
    for i, (src, dst) in enumerate(zip(ins, outs)):
        count = src.shape[0]
        place = dst.at[pl.ds(pl.multiple_of(core * count, 16), count)]
        copies.append(
            pltpu.make_async_remote_copy(
                src, place, send.at[i], recv.at[i], device_id=other, device_id_type=MESH
            )
        )
        copies.append(pltpu.make_async_copy(src, place, local.at[i]))
    for copy in copies:
        copy.start()
    for copy in copies:
        copy.wait()


def run_gather(parts):
    return pl.pallas_call(
        gather_kernel,
        out_shape=[jax.ShapeDtypeStruct((2 * p.shape[0], p.shape[1]), p.dtype) for p in parts],
        in_specs=[pl.BlockSpec(memory_space=pl.ANY)] * 5,
        out_specs=vmem(5),
        scratch_shapes=[pltpu.SemaphoreType.DMA((5,))] * 3,
        compiler_params=params(collective_id=1, has_side_effects=True),
    )(*parts)


def sum_kernel(g, o, st, rc, one, two, zr, cs_, cr, cl, s1, r1, s2, r2, sz, rz, sg, rg, sh, rh):
    section, core, replica = (lax.axis_index(a) for a in ("section", "shard", "replica"))
    x, y, z = replica // 8, replica // 2 % 4, replica % 2

    def at(x_, y_, z_):
        return (section, core, x_ * 8 + y_ * 2 + z_)

    x_next, x_prev = at((x + 1) % 4, y, z), at((x + 3) % 4, y, z)
    y_next, y_prev = at(x, (y + 1) % 4, z), at(x, (y + 3) % 4, z)
    z_pair = at(x, y, 1 - z)
    partner = (section, 1 - core, replica)
    first_pos, second_pos = (x, y), (y, x)
    first_dev = ((x_next, x_prev), (y_next, y_prev))
    second_dev = ((y_next, y_prev), (x_next, x_prev))

    barrier = pltpu.get_barrier_semaphore()
    for device in (partner, x_next, x_prev, y_next, y_prev, z_pair):
        pl.semaphore_signal(barrier, inc=1, device_id=device, device_id_type=MESH)
    pl.semaphore_wait(barrier, 6)

    sent = []

    def send(src, dst, send_sem, recv_sem, device):
        copy = pltpu.make_async_remote_copy(
            src, dst, send_sem, recv_sem, device_id=device, device_id_type=MESH
        )
        copy.start()
        sent.append(copy)
        return copy

    def span(start, count):
        return pl.ds(pl.multiple_of(start, 16), count)

    def wide(ref, index):
        return ref[index].astype(F32)

    cross, own = {}, {}
    for k in (2, 1, 3, 0):
        for h in range(2):
            rows = span(HALF * h + P1 * ((first_pos[h] + k) % 4), P1)
            i = h * 4 + k
            cross[h, k] = send(g.at[1 - core, rows], rc.at[i], cs_.at[i], cr.at[i], partner)
            own[h, k] = pltpu.make_async_copy(g.at[core, rows], st.at[i], cl.at[i])
            own[h, k].start()

    def ring(h, buf, sems, recvs, devs, src, n):
        up, down = devs
        half = n // 2

        def go(i, ref, device):
            return send(ref, buf.at[h * 6 + i], sems.at[h * 6 + i], recvs.at[h * 6 + i], device)

        return go, up, down, half

    h1 = P1 // 2
    first = {}
    for k in (2, 1, 3):
        for h in range(2):
            go, up, down, _ = ring(h, one, s1, r1, first_dev[h], None, P1)
            cross[h, k].wait_recv()
            own[h, k].wait()
            i = h * 4 + k
            st[i] = (wide(st, i) + wide(rc, i)).astype(BF16)
            if k == 2:
                first[h, 0] = go(0, st.at[i, :h1], up)
                first[h, 1] = go(1, st.at[i, h1:], down)
            elif k == 1:
                first[h, 2] = go(2, st.at[i, h1:], up)
            else:
                first[h, 3] = go(3, st.at[i, :h1], down)
    for h in range(2):
        go, up, down, _ = ring(h, one, s1, r1, first_dev[h], None, P1)
        first[h, 0].wait_recv()
        st[h * 4 + 1, :h1] = (st[h * 4 + 1, :h1].astype(F32) + wide(one, h * 6)).astype(BF16)
        first[h, 4] = go(4, st.at[h * 4 + 1, :h1], up)
        first[h, 1].wait_recv()
        st[h * 4 + 3, h1:] = (st[h * 4 + 3, h1:].astype(F32) + wide(one, h * 6 + 1)).astype(BF16)
        first[h, 5] = go(5, st.at[h * 4 + 3, h1:], down)

    h2 = P2 // 2
    second = {}

    def piece(h, k):
        return P2 * ((second_pos[h] + k) % 4)

    for h in range(2):
        cross[h, 0].wait_recv()
        own[h, 0].wait()
        i = h * 4
        first[h, 3].wait_recv()
        first[h, 4].wait_recv()
        st[i, :h1] = (
            st[i, :h1].astype(F32)
            + rc[i, :h1].astype(F32)
            + wide(one, h * 6 + 3)
            + wide(one, h * 6 + 4)
        ).astype(BF16)
        first[h, 2].wait_recv()
        first[h, 5].wait_recv()
        st[i, h1:] = (
            st[i, h1:].astype(F32)
            + rc[i, h1:].astype(F32)
            + wide(one, h * 6 + 2)
            + wide(one, h * 6 + 5)
        ).astype(BF16)
        go, up, down, _ = ring(h, two, s2, r2, second_dev[h], None, P2)
        second[h, 0] = go(0, st.at[i, span(piece(h, 2), h2)], up)
        second[h, 1] = go(1, st.at[i, span(piece(h, 2) + h2, h2)], down)
        second[h, 2] = go(2, st.at[i, span(piece(h, 1) + h2, h2)], up)
        second[h, 3] = go(3, st.at[i, span(piece(h, 3), h2)], down)
    for h in range(2):
        go, up, down, _ = ring(h, two, s2, r2, second_dev[h], None, P2)
        i = h * 4
        second[h, 0].wait_recv()
        rows = span(piece(h, 1), h2)
        st[i, rows] = (st[i, rows].astype(F32) + wide(two, h * 6)).astype(BF16)
        second[h, 4] = go(4, st.at[i, rows], up)
        second[h, 1].wait_recv()
        rows = span(piece(h, 3) + h2, h2)
        st[i, rows] = (st[i, rows].astype(F32) + wide(two, h * 6 + 1)).astype(BF16)
        second[h, 5] = go(5, st.at[i, rows], down)
    zed = {}
    for h in range(2):
        i = h * 4
        rows = span(piece(h, 0), h2)
        second[h, 3].wait_recv()
        second[h, 4].wait_recv()
        st[i, rows] = (
            st[i, rows].astype(F32) + wide(two, h * 6 + 3) + wide(two, h * 6 + 4)
        ).astype(BF16)
        rows = span(piece(h, 0) + h2, h2)
        second[h, 2].wait_recv()
        second[h, 5].wait_recv()
        st[i, rows] = (
            st[i, rows].astype(F32) + wide(two, h * 6 + 2) + wide(two, h * 6 + 5)
        ).astype(BF16)
        zed[h] = send(
            st.at[i, span(piece(h, 0) + P3 * (1 - z), P3)], zr.at[h], sz.at[h], rz.at[h], z_pair
        )

    def block(h, k1, k2, part=None):
        start = HALF * h + P1 * ((first_pos[h] + k1) % 4) + piece(h, k2)
        if part is None:
            return o.at[span(start, P2)]
        return o.at[span(start + P3 * ((z + part) % 2), P3)]

    def give(ref, sems, recvs, i, device):
        return send(ref, ref, sems.at[i], recvs.at[i], device)

    back, along = {}, {}
    for h in range(2):
        zed[h].wait_recv()
        here = piece(h, 0) + P3 * z
        start = HALF * h + P1 * first_pos[h] + here
        o[span(start, P3)] = (
            st[h * 4, span(here, P3)].astype(F32) + wide(zr, h)
        ).astype(BF16)
        ref = block(h, 0, 0, 0)
        zed[h] = give(ref, sz, rz, 2 + h, z_pair)
        for d in range(2):
            along[h, d, 0] = give(ref, sg, rg, h * 6 + d * 3, second_dev[h][d])
    for h in range(2):
        zed[h].wait_recv()
        ref = block(h, 0, 0, 1)
        for d in range(2):
            along[h, d, 1] = give(ref, sg, rg, h * 6 + d * 3 + 1, second_dev[h][d])
        for d in range(2):
            back[h, d, 0] = give(block(h, 0, 0), sh, rh, h * 12 + d * 6, first_dev[h][d])
    for h in range(2):
        along[h, 0, 0].wait_recv()
        along[h, 0, 2] = give(block(h, 0, 3, 0), sg, rg, h * 6 + 2, second_dev[h][0])
        along[h, 1, 0].wait_recv()
        along[h, 1, 1].wait_recv()
        along[h, 1, 2] = give(block(h, 0, 1, 1), sg, rg, h * 6 + 5, second_dev[h][1])
        for d in range(2):
            back[h, d, 1] = give(block(h, 0, 1), sh, rh, h * 12 + d * 6 + 1, first_dev[h][d])
        along[h, 0, 1].wait_recv()
        for d in range(2):
            back[h, d, 3] = give(block(h, 0, 3), sh, rh, h * 12 + d * 6 + 3, first_dev[h][d])
    for h in range(2):
        along[h, 0, 2].wait_recv()
        along[h, 1, 2].wait_recv()
        for d in range(2):
            back[h, d, 2] = give(block(h, 0, 2), sh, rh, h * 12 + d * 6 + 2, first_dev[h][d])
    ahead = {}
    for k in (0, 1, 3, 2):
        for h in range(2):
            back[h, 0, k].wait_recv()
            back[h, 1, k].wait_recv()
            if k in (0, 3):
                ahead[h, k] = give(
                    block(h, 3, k), sh, rh, h * 12 + 4 + (k == 3), first_dev[h][0]
                )
            else:
                ahead[h, k] = give(
                    block(h, 1, k), sh, rh, h * 12 + 10 + (k == 2), first_dev[h][1]
                )
    for copy in ahead.values():
        copy.wait_recv()
    for copy in sent:
        copy.wait_send()


def run_sum(flat):
    dma = pltpu.SemaphoreType.DMA
    return pl.pallas_call(
        sum_kernel,
        out_shape=jax.ShapeDtypeStruct((FLAT, 128), BF16),
        in_specs=[pl.BlockSpec(memory_space=pl.ANY)],
        out_specs=vmem(1)[0],
        scratch_shapes=[
            pltpu.VMEM((8, P1, 128), BF16),
            pltpu.VMEM((8, P1, 128), BF16),
            pltpu.VMEM((12, P1 // 2, 128), BF16),
            pltpu.VMEM((12, P2 // 2, 128), BF16),
            pltpu.VMEM((2, P3, 128), BF16),
            dma((8,)),
            dma((8,)),
            dma((8,)),
            dma((12,)),
            dma((12,)),
            dma((12,)),
            dma((12,)),
            dma((4,)),
            dma((4,)),
            dma((12,)),
            dma((12,)),
            dma((24,)),
            dma((24,)),
        ],
        compiler_params=params(collective_id=2, has_side_effects=True),
    )(flat)


def unpack_kernel(f, gain_one, wq, wk, wv, wo, gain_two, wg, wu, wd):
    def rows(start, count=OWN):
        return f[start : start + count].astype(F32)

    for b in range(12):
        cols = slice(128 * b, 128 * b + 128)
        wg[0, :, cols] = rows(GATE + b * OWN)
        wu[0, :, cols] = rows(UP + b * OWN)
    for b in range(6):
        wd[0, 128 * b : 128 * b + 128, :] = rows(DOWN + b * D, D).T
    for b in range(4):
        wq[0, :, 128 * b : 128 * b + 128] = rows(QKV + b * OWN)
        wo[0, :, 128 * b : 128 * b + 128] = rows(OUT + b * OWN)
    swap = [pltpu.roll(rows(QKV + b * OWN), 64, 1) for b in range(4, 8)]
    wq[0, :, 512:576] = rows(QKV + 4 * OWN)[:, :64]
    lane = lax.broadcasted_iota(jnp.int32, (OWN, 128), 1)
    wk[0, :, :128] = jnp.where(lane < 64, swap[0], swap[1])
    wk[0, :, 128:] = swap[1][:, :64]
    wv[0, :, :128] = rows(QKV + 6 * OWN)
    wv[0, :, 128:] = rows(QKV + 7 * OWN)[:, :64]
    wo[0, :, 512:576] = swap[3][:, :64]
    gains = rows(GAIN).T
    gain_one[...] = gains[0:1]
    gain_two[...] = gains[1:2]


def run_unpack(flat):
    kinds = [(1, OWN), (1, OWN, D), (1, OWN, 192), (1, OWN, 192), (1, OWN, D)]
    kinds += [(1, OWN), (1, OWN, FF), (1, OWN, FF), (1, FF // 2, D)]
    return pl.pallas_call(
        unpack_kernel,
        out_shape=[jax.ShapeDtypeStruct(k, F32) for k in kinds],
        in_specs=vmem(1),
        out_specs=vmem(9),
        compiler_params=params(),
    )(flat)


def over(value, by):
    return lax.ppermute(value, "section", [(0, 1)] if by > 0 else [(1, 0)])


def shards(
    tokens,
    cotangent,
    seq_lengths,
    gain_attn,
    w_query,
    w_key,
    w_value,
    w_out,
    gain_ffn,
    w_gate,
    w_up,
    w_down,
):
    first = lax.axis_index("section") == 0
    side = jnp.concatenate(
        [
            w_query[0],
            w_key[0],
            w_value[0],
            gain_attn[0][:, None],
            gain_ffn[0][:, None],
            jnp.zeros((OWN, 62), BF16),
        ],
        axis=1,
    )
    weights = run_gather([side, w_out[0], w_gate[0], w_up[0], w_down[0]])
    early = run_forward(seq_lengths, tokens, weights)
    layer_in = jnp.where(first, tokens, over(early, 1))
    result, d_early, saved = run_middle(seq_lengths, layer_in, cotangent, weights)
    received = over(d_early, -1)
    d_input, flat = run_last(seq_lengths, layer_in, cotangent, received, weights, saved)
    grads = run_unpack(run_sum(flat))
    return (result[None], d_input[None], *grads)


def solution(mesh):
    row_spec = P(None, ("shard", "replica"), None)
    out_spec = P("section", None, ("shard", "replica"), None)
    vector = P("section", "shard")
    matrix = P("section", "shard", None)
    weight_specs = (vector, matrix, matrix, matrix, matrix, vector, matrix, matrix, matrix)
    return jax.shard_map(
        shards,
        mesh=mesh,
        in_specs=(row_spec, row_spec, P(None, ("shard", "replica")), *weight_specs),
        out_specs=(out_spec, out_spec, *weight_specs),
        check_vma=False,
    )
```

time: 636 us -> 159 us (0.25); the launches traced: 627 us -> 159 us
  waiting for transfers between devices: 239 us -> 15.6 us
  matrix products: 156 us -> 0 us
  Pallas kernels: 0 us -> 119 us
  blocking collectives: 89.5 us -> 0 us
  other arithmetic: 47.2 us -> 0.77 us
  starting transfers between devices: 43 us -> 7.56 us
  local copies, waits for them, and re-layouts: 36.5 us -> 15 us
  between operations: 16.6 us -> 0.77 us
    psum x1 -> x0, waiting for transfers between devices: 212 us -> none  [shards(): lax.psum(as_sent(grouped), 'replica')]
    dot_general x99 -> x0, matrix products: 151 us -> none  [the longest x6 14.7 us: forward_parts(): gate_val = jnp.dot(second, w_gate, preferred_element_type=jnp.float32)]
    pallas_call x0 -> x6, Pallas kernels: none -> 119 us  [the longest x1 61.6 us: run_sum(): pl.pallas_call(sum_kernel, out_shape=jax.ShapeDtypeStruct((FLAT, 128), BF...]
    psum x1 -> x0, blocking collectives: 82.1 us -> none  [shards(): lax.psum(as_sent(grouped), 'replica')]
    all_to_all x7 -> x0, starting transfers between devices: 27.9 us -> none  [summed_on_arrival(): lax.all_to_all(cut_along(shard, dim, length), axis, 0, 0, tiled=True)]
    convert_element_type x30 -> x0, other arithmetic: 19.4 us -> none  [the longest x7 9.23 us: shards(): part.astype(jnp.float32)]
    all_gather x2 -> x0, waiting for transfers between devices: 17.1 us -> none  [the longest x1 13.8 us: side_by_side(): result = lax.all_gather(both, axis, axis=dim, tiled=True)]
    reduce_sum x17 -> x0, other arithmetic: 13.2 us -> none  [the longest x9 11.8 us: summed_on_arrival(): return jnp.sum(blocks.astype(jnp.float32), axis=0)]
  transfers between devices with their start and end apart: 14 -> 2, of which waited for: 9 -> 2; matrix products, arithmetic and copies ran while one was open for 16% -> 2% of each run, Pallas kernels for 0% -> 0%
where the time goes in v1:
time: 159 us
  Pallas kernels  119 us (75%)
  waiting for transfers between devices  15.6 us (10%)
  local copies, waits for them, and re-layouts  15 us (9%)
  starting transfers between devices  7.56 us (5%)
    pallas_call x1, Pallas kernels, run_sum(): pl.pallas_call(sum_kernel, out_shape=jax.ShapeDtypeStruct((FLAT, 128), BF...  61.6 us
    pallas_call x1, Pallas kernels, run_last(): pl.pallas_call(last_kernel, out_shape=[ROW_SHAPE, jax.ShapeDtypeStruct((2...  16.6 us
    pallas_call x1, Pallas kernels, run_middle(): pl.pallas_call(middle_kernel, out_shape=[ROW_SHAPE, ROW_SHAPE] + shapes(S...  16.4 us
    ppermute x2, waiting for transfers between devices, over(): return lax.ppermute(value, 'section', [(0, 1)] if by > 0 else [(1, 0)])  15.6 us
    unnamed x18, local copies, waits for them, and re-layouts  12.2 us
    pallas_call x1, Pallas kernels, run_gather(): pl.pallas_call(gather_kernel, out_shape=[jax.ShapeDtypeStruct((2 * p.shap...  9.79 us
    pallas_call x1, Pallas kernels, run_forward(): pl.pallas_call(forward_kernel, out_shape=ROW_SHAPE, in_specs=smem() + vme...  9.11 us
    ppermute x2, starting transfers between devices, over(): return lax.ppermute(value, 'section', [(0, 1)] if by > 0 else [(1, 0)])  7.56 us
  transfers between devices with their start and end apart: 2, of which 2 were waited for; matrix products, arithmetic and copies ran while one was open for 2% of the time, Pallas kernels for 0%

profile of v1, /device:TPU:0, one launch (start us, length us, event | category | flops | bytes accessed | tf_op | source)
XLA Modules:
  0.0 158.8 jit_solution(8437283059336796744)
XLA Ops:
  0.6 0.0 copy-start.5
  0.7 0.0 copy-start.4
  0.7 0.0 copy-start.1
  0.7 0.9 copy.31
  1.6 0.8 copy.32
  2.4 1.9 %copy.35.x_ref = bf16[2,128,576]{2,1,0:T(8,128)(2,1)} copy(bf16[2,128,576]{1,2,0:T(8,128)(2,1)} %param.12) | data formatting | bytes 589824 | tf_op args[0]
  4.3 2.2 %copy.33 = bf16[1,768,576]{2,1,0:T(8,128)(2,1)} copy(bf16[1,768,576]{1,2,0:T(8,128)(2,1)} %param.23) | data formatting | bytes 1769472 | tf_op args[11]
  6.5 0.0 copy-done.5
  6.5 0.0 copy-done.4
  6.5 0.0 copy-done.1
  6.5 1.1 concatenate.3.refs_0_
  7.6 9.8 %shard_map.203 = (bf16[576,1024]{1,0:T(8,128)(2,1)}, bf16[576,576]{1,0:T(8,128)(2,1)}, bf16[576,1536]{1,0:T(8,128)(2,1)}, bf16[576,1536]{1,0:T(8,128)(2,1)}, bf16[1536,576]{1,0:T(8,128)(2,1)}) custom-call(bf16[288,1024]{1,0:T(8,128)(2,1)} %concatenate.3.refs_0_, bf16[288,576]{1,0:T(8,128)(2,1)} %bitcast.14, bf16[288,1536]{1,0:T(8,128)(2,1)} %bitcast.12, ...), custom_call_target="tpu_custom_call" | custom-call | tf_op jit(solution)/shard_map/pallas_call | solution.py:426
  17.4 0.0 copy-start.3
  17.4 0.0 copy-start
  17.5 9.1 %shard_map.204 = bf16[2,128,576]{2,1,0:T(8,128)(2,1)} custom-call(s32[2,2]{1,0:T(2,128)} %lens.5, bf16[2,128,576]{2,1,0:T(8,128)(2,1)} %copy.35.x_ref, bf16[576,1024]{1,0:T(8,128)(2,1)} %get-tuple-element.42.wq, bf16[576,576]{1,0:T(8,128)(2,1)} %get-tuple-element.43.wo, bf16[576,1536]{1,0:T(8,128)(2,1)} %get-tuple-element.44.wg, ...), custom_call_target="tpu_custom_call" | custom-call | tf_op jit(solution)/shard_map/pallas_call | solution.py:368
  26.6 6.1 %collective-permute-start = (bf16[2,128,576]{2,1,0:T(8,128)(2,1)}, bf16[2,128,576]{2,1,0:T(8,128)(2,1)S(1)}, u32[]{:S(2)}, u32[]{:S(2)}) collective-permute-start(bf16[2,128,576]{2,1,0:T(8,128)(2,1)} %shard_map.204), channel_id=1, source_target_pairs={{0,64},{1,65},{2,66},{3,67},{4,68},{5,69},{6,70},{7,71},{8,72},{9,... | collective-permute-start | bytes 884744 | tf_op jit(solution)/shard_map/ppermute | solution.py:709
  32.6 0.0 copy-done.3
  32.6 0.9 copy.36.cot
  33.5 6.5 %collective-permute-done = bf16[2,128,576]{2,1,0:T(8,128)(2,1)S(1)} collective-permute-done((bf16[2,128,576]{2,1,0:T(8,128)(2,1)}, bf16[2,128,576]{2,1,0:T(8,128)(2,1)S(1)}, u32[]{:S(2)}, u32[]{:S(2)}) %collective-permute-start) | collective-permute-done | bytes 294944 | tf_op jit(solution)/shard_map/ppermute | solution.py:709
  40.0 0.0 copy-done
  40.0 0.8 broadcast_select_fusion.x_ref
  40.8 16.4 %shard_map.205 = (bf16[2,128,576]{2,1,0:T(8,128)(2,1)}, bf16[2,128,576]{2,1,0:T(8,128)(2,1)}, bf16[256,576]{1,0:T(8,128)(2,1)}, bf16[6,384,128]{2,1,0:T(8,128)(2...) custom-call(s32[2,2]{1,0:T(2,128)} %lens.5, ...), custom_call_target="tpu_custom_call" | custom-call | tf_op jit(solution)/shard_map/pallas_call | solution.py:379
  57.1 1.5 collective-permute-start.1
  58.6 1.9 %copy.38 = bf16[1,2,128,576]{2,3,1,0:T(8,128)(2,1)} copy(bf16[1,2,128,576]{3,2,1,0:T(8,128)(2,1)} %bitcast.17) | data formatting | bytes 589824
  60.5 9.2 %collective-permute-done.1.received = bf16[2,128,576]{2,1,0:T(8,128)(2,1)S(1)} collective-permute-done((bf16[2,128,576]{2,1,0:T(8,128)(2,1)}, bf16[2,128,576]{2,1,0:T(8,128)(2,1)S(1)}, u32[]{:S(2)}, u32[]{:S(2)}) %collective-permute-start.1) | collective-permute-done | bytes 294944 | tf_op jit(solution)/shard_map/ppermute | solution.py:709
  69.7 0.0 copy-start.2
  69.7 0.7 copy-done.2
  70.4 16.6 %shard_map.206 = (bf16[2,128,576]{2,1,0:T(8,128)(2,1)}, bf16[2,14336,128]{2,1,0:T(8,128)(2,1)}) custom-call(s32[2,2]{1,0:T(2,128)} %lens.5, bf16[2,128,576]{2,1,0:T(8,128)(2,1)} %broadcast_select_fusion.x_ref, bf16[2,128,576]{2,1,0:T(8,128)(2,1)} %copy.36.cot, bf16[2,128,576]{2,1,0:T(8,128)(2,1)} %copy-done.2, bf16[576,1024]{1,0:T(8,128)(2,1)} %get-tuple-element.42.wq, ...), custom_call_target="tpu_custom_call" | custom-call | tf_op jit(solution)/shard_map/pallas_call | solution.py:391
  87.0 1.9 %copy.39 = bf16[1,2,128,576]{2,3,1,0:T(8,128)(2,1)} copy(bf16[1,2,128,576]{3,2,1,0:T(8,128)(2,1)} %bitcast.16) | data formatting | bytes 589824
  88.9 61.6 %shard_map.207.f = bf16[14336,128]{1,0:T(8,128)(2,1)} custom-call(bf16[2,14336,128]{2,1,0:T(8,128)(2,1)} %get-tuple-element.63.g), custom_call_target="tpu_custom_call" | custom-call | tf_op jit(solution)/shard_map/pallas_call | solution.py:641
  150.5 5.6 %shard_map.208 = (f32[1,288]{1,0:T(1,128)}, f32[1,288,576]{2,1,0:T(8,128)}, f32[1,288,192]{2,1,0:T(8,128)}, f32[1,288,192]{2,1,0:T(8,128)}, f32[1,288,576]{2,1,0...) custom-call(bf16[14336,128]{1,0:T(8,128)(2,1)} %shard_map.207.f), custom_call_target="tpu_custom_call" | custom-call | tf_op jit(solution)/shard_map/pallas_call | solution.py:699
  156.1 2.8 %copy.40 = f32[1,768,576]{1,2,0:T(8,128)} copy(f32[1,768,576]{2,1,0:T(8,128)} %get-tuple-element.94) | data formatting | bytes 3538944
  (1 shorter events, 0.0 us)
Async XLA Ops:
  0.6 5.8 %copy-start.5 = (bf16[1,288,192]{2,1,0:T(8,128)(2,1)S(1)}, bf16[1,288,192]{2,1,0:T(8,128)(2,1)}, u32[]{:S(2)}) copy-start(bf16[1,288,192]{2,1,0:T(8,128)(2,1)} %param.18) | copy-start | bytes 331780
  0.7 5.8 %copy-start.4 = (bf16[1,288,192]{2,1,0:T(8,128)(2,1)S(1)}, bf16[1,288,192]{2,1,0:T(8,128)(2,1)}, u32[]{:S(2)}) copy-start(bf16[1,288,192]{2,1,0:T(8,128)(2,1)} %param.17) | copy-start | bytes 331780
  0.7 5.8 %copy-start.1 = (bf16[1,288,576]{2,1,0:T(8,128)(2,1)S(1)}, bf16[1,288,576]{2,1,0:T(8,128)(2,1)}, u32[]{:S(2)}) copy-start(bf16[1,288,576]{2,1,0:T(8,128)(2,1)} %param.16) | copy-start | bytes 995332
  17.4 15.2 %copy-start.3 = (bf16[2,128,576]{1,2,0:T(8,128)(2,1)S(1)}, bf16[2,128,576]{1,2,0:T(8,128)(2,1)}, u32[]{:S(2)}) copy-start(bf16[2,128,576]{1,2,0:T(8,128)(2,1)} %param.13) | copy-start | bytes 884740
  17.4 22.6 %copy-start = (bf16[2,128,576]{2,1,0:T(8,128)(2,1)S(1)}, bf16[2,128,576]{2,1,0:T(8,128)(2,1)}, u32[]{:S(2)}) copy-start(bf16[2,128,576]{2,1,0:T(8,128)(2,1)} %copy.35.x_ref) | copy-start | bytes 884740
  26.6 13.4 %collective-permute-start = (bf16[2,128,576]{2,1,0:T(8,128)(2,1)}, bf16[2,128,576]{2,1,0:T(8,128)(2,1)S(1)}, u32[]{:S(2)}, u32[]{:S(2)}) collective-permute-start(bf16[2,128,576]{2,1,0:T(8,128)(2,1)} %shard_map.204), channel_id=1, source_target_pairs={{0,64},{1,65},{2,66},{3,67},{4,68},{5,69},{6,70},{7,71},{8,72},{9,... | collective-permute-start | bytes 884744 | tf_op jit(solution)/shard_map/ppermute | solution.py:709
  57.1 12.6 %collective-permute-start.1 = (bf16[2,128,576]{2,1,0:T(8,128)(2,1)}, bf16[2,128,576]{2,1,0:T(8,128)(2,1)S(1)}, u32[]{:S(2)}, u32[]{:S(2)}) collective-permute-start(bf16[2,128,576]{2,1,0:T(8,128)(2,1)} %get-tuple-element.48), channel_id=1, source_target_pairs={{64,0},{65,1},{66,2},{67,3},{68,4},{69,5},{70,6},{71,7},{72,8},{73... | collective-permute-start | bytes 884744 | tf_op jit(solution)/shard_map/ppermute | solution.py:709
  69.7 0.7 copy-start.2

commit v2 on v0

v2 whole, which is shorter than its diff:
```python
import functools
import math

import jax
import jax.numpy as jnp
from jax import lax
from jax.experimental import pallas as pl
from jax.experimental.pallas import tpu as pltpu
from jax.sharding import PartitionSpec as P

MESH = pl.DeviceIdType.MESH
F32 = jnp.float32
BF16 = jnp.bfloat16

D = 576
HD = 64
FF = 1536
ROWS = 128
MICRO = 2
M = MICRO * ROWS
OWN = D // 2
EPS = 1e-05
BASE = 100000.0
VMEM_LIMIT = 62 * 1024 * 1024

GATE = 0
UP = GATE + 12 * OWN
DOWN = UP + 12 * OWN
QKV = DOWN + 6 * D
OUT = QKV + 8 * OWN
GAIN = OUT + 4 * OWN
USED = GAIN + OWN
FLAT = 14336
HALF = FLAT // 2
P1 = HALF // 4
P2 = P1 // 4
P3 = P2 // 2


def dot(a, b):
    return lax.dot_general(a, b, (((1,), (0,)), ((), ())), preferred_element_type=F32)


def dot_nt(a, b):
    return lax.dot_general(a, b, (((1,), (1,)), ((), ())), preferred_element_type=F32)


def dot_tn(a, b):
    return lax.dot_general(a, b, (((0,), (0,)), ((), ())), preferred_element_type=F32)


def lanes():
    return lax.broadcasted_iota(jnp.int32, (ROWS, 128), 1)


def slots():
    return lax.broadcasted_iota(jnp.int32, (ROWS, 128), 0)


def segment_of(ids, first_end, last_end):
    return jnp.where(ids >= first_end, 1, 0) + jnp.where(ids >= last_end, 1, 0)


def turned(u, lane):
    return jnp.where(lane % 64 < 32, pltpu.roll(u, 96, 1), pltpu.roll(u, 32, 1))


def both_halves(u, half, lane):
    return jnp.where(lane // 64 == half, u, pltpu.roll(u, 64, 1))


def norm_scale(x):
    return lax.rsqrt(jnp.mean(x * x, axis=-1, keepdims=True) + EPS)


def norm_back(upper, normed, scale):
    return scale * (upper - normed * jnp.mean(upper * normed, axis=-1, keepdims=True))


def lengths_of(r, m):
    first = r["lens"][m, 0:1, 0:1].astype(jnp.int32)
    return first, first + r["lens"][m, 0:1, 1:2].astype(jnp.int32)


def tables(r, m):
    first_end, last_end = lengths_of(r, m)
    lane, slot = lanes(), slots()
    inverse = jnp.exp((lane % 32).astype(F32) * (-2.0 * math.log(BASE) / HD))
    position = slot - jnp.where(slot >= first_end, first_end, 0)
    position = position - jnp.where(slot >= last_end, last_end - first_end, 0)
    angle = position.astype(F32) * inverse
    sine = jnp.sin(angle)
    r["cs"][m] = jnp.cos(angle)
    r["sn"][m] = jnp.where(lane % 64 < 32, -sine, sine)


def side_rows(wq, wk, wv, gain_one, gain_two):
    lane = lax.broadcasted_iota(jnp.int32, (OWN, 128), 1)
    none = jnp.zeros((OWN, 64), F32)
    tail = jnp.concatenate([wq[:, 512:576].astype(F32), none], axis=1)
    key_a = pltpu.roll(wk[:, :128].astype(F32), 64, 1)
    key_b = pltpu.roll(jnp.concatenate([wk[:, 128:192].astype(F32), none], axis=1), 64, 1)
    last = jnp.concatenate([wv[:, 128:192].astype(F32), none], axis=1)
    row = lax.broadcasted_iota(jnp.int32, (128, OWN), 0)
    gains = jnp.where(
        row == 64, gain_one[...].astype(F32), jnp.where(row == 65, gain_two[...].astype(F32), 0.0)
    ).T
    return {
        512: jnp.where(lane < 64, tail, key_a),
        640: jnp.where(lane < 64, key_a, key_b),
        768: wv[:, :128].astype(F32),
        896: last + gains,
    }


def forward(r, m, arrived):
    tables(r, m)
    x = r["x"][m]
    arrived("side")
    wq, wo, wg, wu, wd = (r[k] for k in ("wq", "wo", "wg", "wu", "wd"))
    gains = wq[:, 896:1024].astype(F32).T
    g1, g2 = gains[64:65], gains[65:66]
    entry = (x * norm_scale(x) * g1).astype(BF16)
    r["ent"][m] = entry
    qkv = dot(entry, wq[...])
    lane = lanes()
    cosine, sine = r["cs"][m], r["sn"][m]
    first_end, last_end = lengths_of(r, m)
    allowed = (
        segment_of(slots(), first_end, last_end) == segment_of(lane, first_end, last_end)
    ) & (lane <= slots())
    allowed = jnp.concatenate([allowed.astype(F32)] * 3, axis=0) > 0.5
    blocks = []
    for b in range(6):
        u = qkv[:, 128 * b : 128 * b + 128]
        blocks.append(u * cosine + turned(u, lane) * sine)
    heads = []
    for kv in range(3):
        kj = 9 + kv
        key = both_halves(blocks[kj // 2], kj % 2, lane).astype(BF16)
        vb = qkv[:, 768 + 128 * (kv // 2) : 896 + 128 * (kv // 2)]
        value = both_halves(vb, kv % 2, lane).astype(BF16)
        query = jnp.concatenate(
            [
                jnp.where(lane // 64 == j % 2, blocks[j // 2], 0.0).astype(BF16)
                for j in range(3 * kv, 3 * kv + 3)
            ],
            axis=0,
        )
        r["kd"][m, kv] = key
        r["vd"][m, kv] = value
        r["qs"][m, kv] = query
        scores = jnp.where(allowed, dot_nt(query, key) * HD**-0.5, -1e30)
        weights = jnp.exp(scores - jnp.max(scores, axis=-1, keepdims=True))
        probs = weights / jnp.sum(weights, axis=-1, keepdims=True)
        r["pr"][m, kv] = probs
        out = dot(probs.astype(BF16), value)
        heads += [out[ROWS * g : ROWS * (g + 1)] for g in range(3)]
    for b in range(4):
        r["mix"][m, :, 128 * b : 128 * b + 128] = jnp.where(
            lane < 64, heads[2 * b], heads[2 * b + 1]
        ).astype(BF16)
    r["mix"][m, :, 512:576] = heads[8][:, :64].astype(BF16)
    arrived("wo")
    middle = x + dot(r["mix"][m], wo[...])
    r["mid"][m] = middle
    second = (middle * norm_scale(middle) * g2).astype(BF16)
    r["sec"][m] = second
    arrived("wg")
    arrived("wu")
    for j in range(0, FF, 256):
        cols = slice(j, j + 256)
        gate = dot(second, wg[:, cols])
        up = dot(second, wu[:, cols])
        sig = 1.0 / (1.0 + jnp.exp(-gate))
        swish = gate * sig
        r["inn"][m, :, cols] = (swish * up).astype(BF16)
        r["fa"][m, :, cols] = up * sig * (1.0 + gate * (1.0 - sig))
        r["fb"][m, :, cols] = swish
    arrived("wd")
    return middle + dot_nt(r["inn"][m], wd[...])


def backward(r, m):
    wq, wo, wg, wu, wd = (r[k] for k in ("wq", "wo", "wg", "wu", "wd"))
    gains = wq[:, 896:1024].astype(F32).T
    g1, g2 = gains[64:65], gains[65:66]
    dy = r["dy"][m]
    middle = r["mid"][m]
    scale_two = norm_scale(middle)
    n2 = middle * scale_two
    df = dy.astype(BF16)
    r["df"][m] = df
    for j in range(0, FF, 256):
        cols = slice(j, j + 256)
        d_inner = dot(df, wd[:, cols])
        r["dg"][m, :, cols] = (d_inner * r["fa"][m, :, cols]).astype(BF16)
        r["du"][m, :, cols] = (d_inner * r["fb"][m, :, cols]).astype(BF16)
    d_second = dot_nt(r["dg"][m], wg[...]) + dot_nt(r["du"][m], wu[...])
    r["gsum"][m, 1:2, :] = jnp.sum(d_second * n2, axis=0, keepdims=True)
    d_middle = dy + norm_back(d_second * g2, n2, scale_two)
    branch = d_middle.astype(BF16)
    r["db"][m] = branch
    d_mixed = dot_nt(branch, wo[...])
    lane = lanes()
    cosine, sine = r["cs"][m], r["sn"][m]
    dq, dk, dv = [], [], []
    for kv in range(3):
        parts = []
        for j in range(3 * kv, 3 * kv + 3):
            if j < 8:
                block = d_mixed[:, 128 * (j // 2) : 128 * (j // 2) + 128]
                block = jnp.where(lane // 64 == j % 2, block, 0.0)
            else:
                block = jnp.concatenate([d_mixed[:, 512:576], jnp.zeros((ROWS, 64), F32)], axis=1)
            parts.append(block.astype(BF16))
        upper = jnp.concatenate(parts, axis=0)
        probs = r["pr"][m, kv]
        d_probs = dot_nt(upper, r["vd"][m, kv])
        value = dot_tn(probs.astype(BF16), upper)
        dv.append(value + pltpu.roll(value, 64, 1))
        total = jnp.sum(d_probs * probs, axis=-1, keepdims=True)
        d_scores = (probs * (d_probs - total) * HD**-0.5).astype(BF16)
        query = dot(d_scores, r["kd"][m, kv])
        dq += [query[ROWS * g : ROWS * (g + 1)] for g in range(3)]
        key = dot_tn(d_scores, r["qs"][m, kv])
        dk.append(key + pltpu.roll(key, 64, 1))
    heads = dq + dk
    for b in range(6):
        u = jnp.where(lane < 64, heads[2 * b], heads[2 * b + 1])
        r["dqkv"][m, :, 128 * b : 128 * b + 128] = (u * cosine - turned(u, lane) * sine).astype(
            BF16
        )
    r["dqkv"][m, :, 768:896] = jnp.where(lane < 64, dv[0], dv[1]).astype(BF16)
    r["dqkv"][m, :, 896:1024] = jnp.where(lane < 64, dv[2], 0.0).astype(BF16)
    d_entry = dot_nt(r["dqkv"][m], wq[...])
    x = r["x"][m]
    scale_one = norm_scale(x)
    n1 = x * scale_one
    r["gsum"][m, 0:1, :] = jnp.sum(d_entry * n1, axis=0, keepdims=True)
    return d_middle + norm_back(d_entry * g1, n1, scale_one)


def weight_grads(r, flat, done):
    def whole(name, cols=slice(None)):
        value = r[name][:, :, cols]
        return value.reshape(M, value.shape[-1])

    def store(start, block):
        flat[0, start : start + OWN] = block[:OWN].astype(BF16)
        flat[1, start : start + OWN] = block[OWN:].astype(BF16)
        done(start + OWN)

    second_t = whole("sec").T
    for name, start in (("dg", GATE), ("du", UP)):
        for b in range(0, 12, 2):
            g = dot(second_t, whole(name, slice(128 * b, 128 * b + 256)))
            store(start + b * OWN, g[:, :128])
            store(start + (b + 1) * OWN, g[:, 128:])
    df_t = whole("df").T
    for b in range(6):
        for owner in range(2):
            g = dot(df_t, whole("inn", slice(768 * owner + 128 * b, 768 * owner + 128 * b + 128)))
            flat[owner, DOWN + b * D : DOWN + (b + 1) * D] = g.astype(BF16)
        done(DOWN + (b + 1) * D)
    entry_t = whole("ent").T
    mixed_t = whole("mix").T
    for b in range(0, 8, 2):
        g = dot(entry_t, whole("dqkv", slice(128 * b, 128 * b + 256)))
        store(QKV + b * OWN, g[:, :128])
        if b == 6:
            rest = whole("db", slice(512, 576)).astype(F32)
            rest = jnp.concatenate([rest, jnp.zeros((M, 64), F32)], axis=1)
            rest = pltpu.roll(rest, 64, 1).astype(BF16)
            store(QKV + 7 * OWN, g[:, 128:] + dot(mixed_t, rest))
        else:
            store(QKV + (b + 1) * OWN, g[:, 128:])
    for b in range(0, 4, 2):
        g = dot(mixed_t, whole("db", slice(128 * b, 128 * b + 256)))
        store(OUT + b * OWN, g[:, :128])
        store(OUT + (b + 1) * OWN, g[:, 128:])
    sums = r["gsum"][0] + r["gsum"][1]
    row = lax.broadcasted_iota(jnp.int32, (128, D), 0)
    store(GAIN, jnp.where(row == 0, sums[0:1], jnp.where(row == 1, sums[1:2], 0.0)).T)
    flat[0, USED:] = jnp.zeros((FLAT - USED, 128), BF16)
    flat[1, USED:] = jnp.zeros((FLAT - USED, 128), BF16)
    done(FLAT)


KEPT = {
    "wq": ((D, 1024), BF16),
    "wo": ((D, D), BF16),
    "wg": ((D, FF), BF16),
    "wu": ((D, FF), BF16),
    "wd": ((D, FF), BF16),
    "x": ((MICRO, ROWS, D), F32),
    "dy": ((MICRO, ROWS, D), F32),
    "lens": ((MICRO, 8, 128), F32),
    "lens_own": ((MICRO, 8, 128), F32),
    "lens_pair": ((MICRO, 8, 128), F32),
    "cot_pair": ((MICRO, D, ROWS), BF16),
    "y_send": ((MICRO, ROWS, D), BF16),
    "y_box": ((MICRO, ROWS, D), BF16),
    "y_turn": ((MICRO, D, ROWS), BF16),
    "dx_send": ((MICRO, ROWS, D), BF16),
    "dx_box": ((MICRO, ROWS, D), BF16),
    "dx_turn": ((MICRO, D, ROWS), BF16),
    "ent": ((MICRO, ROWS, D), BF16),
    "qs": ((MICRO, 3, 3 * ROWS, 128), BF16),
    "kd": ((MICRO, 3, ROWS, 128), BF16),
    "vd": ((MICRO, 3, ROWS, 128), BF16),
    "pr": ((MICRO, 3, 3 * ROWS, 128), F32),
    "mix": ((MICRO, ROWS, D), BF16),
    "mid": ((MICRO, ROWS, D), F32),
    "sec": ((MICRO, ROWS, D), BF16),
    "inn": ((MICRO, ROWS, FF), BF16),
    "fa": ((MICRO, ROWS, FF), F32),
    "fb": ((MICRO, ROWS, FF), F32),
    "cs": ((MICRO, ROWS, 128), F32),
    "sn": ((MICRO, ROWS, 128), F32),
    "df": ((MICRO, ROWS, D), BF16),
    "dg": ((MICRO, ROWS, FF), BF16),
    "du": ((MICRO, ROWS, FF), BF16),
    "db": ((MICRO, ROWS, D), BF16),
    "dqkv": ((MICRO, ROWS, 1024), BF16),
    "gsum": ((MICRO, 8, D), F32),
    "flat": ((2, FLAT, 128), BF16),
    "cross": ((8, P1, 128), BF16),
    "one": ((12, P1 // 2, 128), BF16),
    "two": ((12, P2 // 2, 128), BF16),
    "zed": ((2, P3, 128), BF16),
}
SEMS = {
    "w": 5,
    "swap": 2,
    "y": 2,
    "dx": 2,
    "y_swap": 2,
    "dx_swap": 2,
    "cross": 8,
    "one": 12,
    "two": 12,
    "zed": 4,
    "along": 12,
    "back": 24,
}


def vmem(n):
    return [pl.BlockSpec(memory_space=pltpu.VMEM)] * n


def hbm(n):
    return [pl.BlockSpec(memory_space=pl.ANY)] * n


def places():
    section, core, replica = (lax.axis_index(a) for a in ("section", "shard", "replica"))
    x, y, z = replica // 8, replica // 2 % 4, replica % 2

    def at(x_, y_, z_):
        return (section, core, x_ * 8 + y_ * 2 + z_)

    return {
        "section": section,
        "core": core,
        "x": x,
        "y": y,
        "z": z,
        "x_next": at((x + 1) % 4, y, z),
        "x_prev": at((x + 3) % 4, y, z),
        "y_next": at(x, (y + 1) % 4, z),
        "y_prev": at(x, (y + 3) % 4, z),
        "z_pair": at(x, y, 1 - z),
        "partner": (section, 1 - core, replica),
        "across": (1 - section, core, x * 8 + y * 2 + (1 - z)),
    }


def step_kernel(
    lens, tok, cot, gain_one, gain_two, wq_own, wk_own, wv_own, wo_own, wg_own, wu_own, wd_own,
    y_out, dx_out, o, *refs
):
    r = dict(zip(KEPT, refs))
    sends = dict(zip(SEMS, refs[len(KEPT) :]))
    recvs = dict(zip(SEMS, refs[len(KEPT) + len(SEMS) :]))
    local = refs[len(KEPT) + 2 * len(SEMS)]
    at = places()
    section, core = at["section"], at["core"]

    barrier = pltpu.get_barrier_semaphore()
    near = ("partner", "x_next", "x_prev", "y_next", "y_prev", "z_pair", "across")
    for name in near:
        pl.semaphore_signal(barrier, inc=1, device_id=at[name], device_id_type=MESH)
    pl.semaphore_wait(barrier, len(near))

    def remote(name, i, src, dst, device):
        return pltpu.make_async_remote_copy(
            src,
            dst,
            sends[name].at[i],
            recvs[name].at[i],
            device_id=at[device],
            device_id_type=MESH,
        )

    own_rows = pl.ds(pl.multiple_of(core * OWN, 16), OWN)
    own_cols = pl.ds(pl.multiple_of(core * (FF // 2), 128), FF // 2)
    weight_places = {
        "wo": (wo_own, r["wo"].at[own_rows]),
        "wg": (wg_own, r["wg"].at[own_rows]),
        "wu": (wu_own, r["wu"].at[own_rows]),
        "wd": (wd_own, r["wd"].at[:, own_cols]),
    }
    r["wq"][own_rows, :512] = wq_own[:, :512]
    for start, value in side_rows(wq_own, wk_own, wv_own, gain_one, gain_two).items():
        r["wq"][own_rows, start : start + 128] = value.astype(BF16)
    side_place = r["wq"].at[own_rows]
    weight_copies = {"side": [remote("w", 0, side_place, side_place, "partner")]}
    for i, (name, (src, dst)) in enumerate(weight_places.items()):
        weight_copies[name] = [
            remote("w", i + 1, src, dst, "partner"),
            pltpu.make_async_copy(src, dst, local.at[i]),
        ]
    for copies in weight_copies.values():
        for copy in copies:
            copy.start()

    r["lens_own"][...] = jnp.zeros((MICRO, 8, 128), F32)
    for m in range(MICRO):
        r["lens_own"][m, 0:1, 0:2] = lens[m : m + 1, :].astype(F32)
    lens_swap = remote("swap", 0, r["lens_own"], r["lens_pair"], "z_pair")
    cot_swap = remote("swap", 1, cot, r["cot_pair"], "z_pair")
    lens_swap.start()
    cot_swap.start()
    lens_swap.wait_recv()

    @pl.when(section == 0)
    def _():
        r["lens"][...] = r["lens_own"][...]

    @pl.when(section == 1)
    def _():
        r["lens"][...] = r["lens_pair"][...]

    def y_copy(m):
        return remote("y", m, r["y_send"].at[m], r["y_box"].at[m], "across")

    def dx_copy(m):
        return remote("dx", m, r["dx_send"].at[m], r["dx_box"].at[m], "across")

    def y_swap(m):
        return remote("y_swap", m, r["y_turn"].at[m], y_out.at[m], "z_pair")

    def dx_swap(m):
        return remote("dx_swap", m, r["dx_turn"].at[m], dx_out.at[m], "z_pair")

    def tick(t, carry):
        m = jnp.where(section == 0, t % 2, t // 2)
        ahead = jnp.where(section == 0, t // 2, t % 2) == 0

        @pl.when(ahead)
        def _():
            @pl.when(section == 0)
            def _():
                r["x"][m] = tok[m].astype(F32).T

            @pl.when(section == 1)
            def _():
                y_copy(m).wait_recv()
                r["x"][m] = r["y_box"][m].astype(F32)

            def arrived(name):
                @pl.when(t == 0)
                def _():
                    for i, copy in enumerate(weight_copies[name]):
                        if i == 0:
                            copy.wait_recv()
                        else:
                            copy.wait()

            y = forward(r, m, arrived)
            r["y_send"][m] = y.astype(BF16)

            @pl.when(section == 0)
            def _():
                y_copy(m).start()
                y_out[m] = r["y_send"][m].astype(F32).T.astype(BF16)

            @pl.when(section == 1)
            def _():
                r["y_turn"][m] = r["y_send"][m].astype(F32).T.astype(BF16)
                y_swap(m).start()

        @pl.when(jnp.logical_not(ahead))
        def _():
            @pl.when(section == 0)
            def _():
                dx_copy(m).wait_recv()
                r["dy"][m] = r["dx_box"][m].astype(F32)

            @pl.when(section == 1)
            def _():
                @pl.when(t == 1)
                def _():
                    cot_swap.wait_recv()

                ids = lax.broadcasted_iota(jnp.int32, (ROWS, D), 0)
                live = ids < lengths_of(r, m)[1]
                r["dy"][m] = jnp.where(live, r["cot_pair"][m].astype(F32).T, 0.0)

            r["dx_send"][m] = backward(r, m).astype(BF16)

            @pl.when(section == 0)
            def _():
                dx_out[m] = r["dx_send"][m].astype(F32).T.astype(BF16)

            @pl.when(section == 1)
            def _():
                dx_copy(m).start()
                r["dx_turn"][m] = r["dx_send"][m].astype(F32).T.astype(BF16)
                dx_swap(m).start()

        return carry

    lax.fori_loop(0, 2 * MICRO, tick, 0)

    @pl.when(section == 0)
    def _():
        cot_swap.wait_recv()

    total = Total(r, o, at, remote)
    weight_grads(r, r["flat"], total.ready)
    total.reduce()
    total.spread()
    total.finish()

    lens_swap.wait_send()
    cot_swap.wait_send()
    for copies in weight_copies.values():
        copies[0].wait_send()

    @pl.when(section == 0)
    def _():
        for m in range(MICRO):
            y_copy(m).wait_send()

    @pl.when(section == 1)
    def _():
        for m in range(MICRO):
            dx_copy(m).wait_send()
            y_swap(m).wait()
            dx_swap(m).wait()


def span(start, count):
    return pl.ds(pl.multiple_of(start, 16), count)


class Total:
    def __init__(self, r, o, at, remote):
        self.flat, self.box, self.one, self.two, self.zed = (
            r[k] for k in ("flat", "cross", "one", "two", "zed")
        )
        self.o, self.at, self.remote = o, at, remote
        self.core, self.z = at["core"], at["z"]
        self.pos = ((at["x"], at["y"]), (at["y"], at["x"]))
        xs, ys = ("x_next", "x_prev"), ("y_next", "y_prev")
        self.dev = ((xs, ys), (ys, xs))
        self.sent, self.cross = [], {}

    def send(self, name, i, src, dst, device):
        copy = self.remote(name, i, src, dst, device)
        copy.start()
        self.sent.append(copy)
        return copy

    def ready(self, rows):
        while len(self.cross) < 8 and P1 * (len(self.cross) + 1) <= rows:
            i = len(self.cross)
            src = self.flat.at[1 - self.core, P1 * i : P1 * (i + 1)]
            self.cross[i] = self.send("cross", i, src, self.box.at[i], "partner")

    def rows(self, h, k, start=0, count=P1):
        return span(HALF * h + P1 * ((self.pos[h][0] + k) % 4) + start, count)

    def add(self, h, k, start, count, *others):
        rows = self.rows(h, k, start, count)
        box = self.box[h * 4 + (self.pos[h][0] + k) % 4, start : start + count]
        value = self.flat[self.core, rows].astype(F32) + box.astype(F32)
        for other in others:
            value = value + other.astype(F32)
        self.flat[self.core, rows] = value.astype(BF16)
        return self.flat.at[self.core, rows]

    def piece(self, h, k):
        return P2 * ((self.pos[h][1] + k) % 4)

    def add_two(self, h, k, start, *others):
        rows = self.rows(h, 0, self.piece(h, k) + start, P2 // 2)
        value = self.flat[self.core, rows].astype(F32)
        for other in others:
            value = value + other.astype(F32)
        self.flat[self.core, rows] = value.astype(BF16)
        return self.flat.at[self.core, rows]

    def reduce(self):
        h1, h2 = P1 // 2, P2 // 2
        one, two = {}, {}

        def go1(h, i, ref, way):
            buf = self.one.at[h * 6 + i]
            one[h, i] = self.send("one", h * 6 + i, ref, buf, self.dev[h][0][way])

        def go2(h, i, ref, way):
            buf = self.two.at[h * 6 + i]
            two[h, i] = self.send("two", h * 6 + i, ref, buf, self.dev[h][1][way])

        def got1(h, i):
            one[h, i].wait_recv()
            return self.one[h * 6 + i]

        def got2(h, i):
            two[h, i].wait_recv()
            return self.two[h * 6 + i]

        for h in range(2):
            for q in range(4):
                self.cross[h * 4 + q].wait_recv()
            go1(h, 0, self.add(h, 2, 0, h1), 0)
            go1(h, 1, self.add(h, 2, h1, h1), 1)
            go1(h, 2, self.add(h, 1, h1, h1), 0)
            go1(h, 3, self.add(h, 3, 0, h1), 1)
        for h in range(2):
            go1(h, 4, self.add(h, 1, 0, h1, got1(h, 0)), 0)
            go1(h, 5, self.add(h, 3, h1, h1, got1(h, 1)), 1)
        for h in range(2):
            self.add(h, 0, 0, h1, got1(h, 3), got1(h, 4))
            self.add(h, 0, h1, h1, got1(h, 2), got1(h, 5))

            def part(k, start):
                return self.flat.at[self.core, self.rows(h, 0, self.piece(h, k) + start, h2)]

            go2(h, 0, part(2, 0), 0)
            go2(h, 1, part(2, h2), 1)
            go2(h, 2, part(1, h2), 0)
            go2(h, 3, part(3, 0), 1)
        for h in range(2):
            go2(h, 4, self.add_two(h, 1, 0, got2(h, 0)), 0)
            go2(h, 5, self.add_two(h, 3, h2, got2(h, 1)), 1)
        self.z_copies = {}
        for h in range(2):
            self.add_two(h, 0, 0, got2(h, 3), got2(h, 4))
            self.add_two(h, 0, h2, got2(h, 2), got2(h, 5))
            rows = self.rows(h, 0, self.piece(h, 0) + P3 * (1 - self.z), P3)
            self.z_copies[h] = self.send(
                "zed", h, self.flat.at[self.core, rows], self.zed.at[h], "z_pair"
            )

    def block(self, h, k1, k2, part=None):
        start = self.piece(h, k2)
        if part is None:
            return self.o.at[self.rows(h, k1, start, P2)]
        return self.o.at[self.rows(h, k1, start + P3 * ((self.z + part) % 2), P3)]

    def spread(self):
        along, back, ahead = {}, {}, {}

        def give(name, i, ref, device):
            return self.send(name, i, ref, ref, device)

        def give_first(h, k):
            for d in range(2):
                back[h, d, k] = give(
                    "back", h * 12 + d * 6 + k, self.block(h, 0, k), self.dev[h][0][d]
                )

        def give_second(h, k):
            for d in range(2):
                along[h, d, k] = give(
                    "along", h * 6 + d * 3 + k, self.block(h, 0, 0, k), self.dev[h][1][d]
                )

        for h in range(2):
            self.z_copies[h].wait_recv()
            rows = self.rows(h, 0, self.piece(h, 0) + P3 * self.z, P3)
            value = self.flat[self.core, rows].astype(F32) + self.zed[h].astype(F32)
            self.o[rows] = value.astype(BF16)
            self.z_copies[h] = give("zed", 2 + h, self.block(h, 0, 0, 0), "z_pair")
            give_second(h, 0)
        for h in range(2):
            self.z_copies[h].wait_recv()
            give_second(h, 1)
            give_first(h, 0)
        for h in range(2):
            along[h, 0, 0].wait_recv()
            along[h, 0, 2] = give("along", h * 6 + 2, self.block(h, 0, 3, 0), self.dev[h][1][0])
            along[h, 1, 0].wait_recv()
            along[h, 1, 1].wait_recv()
            along[h, 1, 2] = give("along", h * 6 + 5, self.block(h, 0, 1, 1), self.dev[h][1][1])
            give_first(h, 1)
            along[h, 0, 1].wait_recv()
            give_first(h, 3)
        for h in range(2):
            along[h, 0, 2].wait_recv()
            along[h, 1, 2].wait_recv()
            give_first(h, 2)
        for k in (0, 1, 3, 2):
            for h in range(2):
                back[h, 0, k].wait_recv()
                back[h, 1, k].wait_recv()
                way = 0 if k in (0, 3) else 1
                ahead[h, k] = give(
                    "back",
                    h * 12 + way * 6 + (4 if k < 2 else 5),
                    self.block(h, 1 if way else 3, k),
                    self.dev[h][0][way],
                )
        for copy in ahead.values():
            copy.wait_recv()

    def finish(self):
        for copy in self.sent:
            copy.wait_send()


def run_step(lens, tok, cot, gain_one, gain_two, wq, wk, wv, wo, wg, wu, wd):
    rows = jax.ShapeDtypeStruct((MICRO, D, ROWS), BF16)
    sems = [pltpu.SemaphoreType.DMA((n,)) for n in SEMS.values()]
    return pl.pallas_call(
        step_kernel,
        out_shape=[rows, rows, jax.ShapeDtypeStruct((FLAT, 128), BF16)],
        in_specs=vmem(8) + hbm(4),
        out_specs=vmem(3),
        scratch_shapes=[pltpu.VMEM(*v) for v in KEPT.values()]
        + sems
        + sems
        + [pltpu.SemaphoreType.DMA((4,))],
        compiler_params=pltpu.CompilerParams(
            collective_id=1, has_side_effects=True, vmem_limit_bytes=VMEM_LIMIT
        ),
    )(lens, tok, cot, gain_one, gain_two, wq, wk, wv, wo, wg, wu, wd)


def unpack_kernel(f, y, dx, y_out, dx_out, gain_one, wq, wk, wv, wo, gain_two, wg, wu, wd):
    def rows(start, count=OWN):
        return f[start : start + count].astype(F32)

    y_out[...] = y[...]
    dx_out[...] = dx[...]
    for b in range(12):
        cols = slice(128 * b, 128 * b + 128)
        wg[0, :, cols] = rows(GATE + b * OWN)
        wu[0, :, cols] = rows(UP + b * OWN)
    for b in range(6):
        wd[0, :, 128 * b : 128 * b + 128] = rows(DOWN + b * D, D)
    for b in range(4):
        wq[0, :, 128 * b : 128 * b + 128] = rows(QKV + b * OWN)
        wo[0, :, 128 * b : 128 * b + 128] = rows(OUT + b * OWN)
    swap = [pltpu.roll(rows(QKV + b * OWN), 64, 1) for b in range(4, 8)]
    wq[0, :, 512:576] = rows(QKV + 4 * OWN)[:, :64]
    lane = lax.broadcasted_iota(jnp.int32, (OWN, 128), 1)
    wk[0, :, :128] = jnp.where(lane < 64, swap[0], swap[1])
    wk[0, :, 128:] = swap[1][:, :64]
    wv[0, :, :128] = rows(QKV + 6 * OWN)
    wv[0, :, 128:] = rows(QKV + 7 * OWN)[:, :64]
    wo[0, :, 512:576] = swap[3][:, :64]
    gains = rows(GAIN).T
    gain_one[...] = gains[0:1]
    gain_two[...] = gains[1:2]


def run_unpack(flat, y, dx):
    kinds = [(1, OWN), (1, OWN, D), (1, OWN, 192), (1, OWN, 192), (1, OWN, D)]
    kinds += [(1, OWN), (1, OWN, FF), (1, OWN, FF), (1, D, FF // 2)]
    return pl.pallas_call(
        unpack_kernel,
        out_shape=[jax.ShapeDtypeStruct(a.shape, a.dtype) for a in (y, dx)]
        + [jax.ShapeDtypeStruct(k, F32) for k in kinds],
        in_specs=vmem(3),
        out_specs=vmem(11),
        compiler_params=pltpu.CompilerParams(vmem_limit_bytes=VMEM_LIMIT),
    )(flat, y, dx)


def shards(
    tokens,
    cotangent,
    seq_lengths,
    gain_attn,
    w_query,
    w_key,
    w_value,
    w_out,
    gain_ffn,
    w_gate,
    w_up,
    w_down,
):
    y, dx, flat = run_step(
        seq_lengths,
        jnp.swapaxes(tokens, 1, 2),
        jnp.swapaxes(cotangent, 1, 2),
        gain_attn,
        gain_ffn,
        w_query[0],
        w_key[0],
        w_value[0],
        w_out[0],
        w_gate[0],
        w_up[0],
        w_down[0].T,
    )
    y, dx, *grads = run_unpack(flat, y, dx)
    grads[8] = jnp.swapaxes(grads[8], 1, 2)
    return (jnp.swapaxes(y, 1, 2)[None], jnp.swapaxes(dx, 1, 2)[None], *grads)


def solution(mesh):
    row_spec = P(None, ("shard", "replica"), None)
    out_spec = P("section", None, ("shard", "replica"), None)
    vector = P("section", "shard")
    matrix = P("section", "shard", None)
    weight_specs = (vector, matrix, matrix, matrix, matrix, vector, matrix, matrix, matrix)
    return jax.shard_map(
        shards,
        mesh=mesh,
        in_specs=(row_spec, row_spec, P(None, ("shard", "replica")), *weight_specs),
        out_specs=(out_spec, out_spec, *weight_specs),
        check_vma=False,
    )
```

time: 636 us -> 114 us (0.18); the launches traced: 627 us -> 114 us
  waiting for transfers between devices: 239 us -> 0 us
  matrix products: 156 us -> 0 us
  Pallas kernels: 0 us -> 113 us
  blocking collectives: 89.5 us -> 0 us
  other arithmetic: 47.2 us -> 0 us
  starting transfers between devices: 43 us -> 0 us
  local copies, waits for them, and re-layouts: 36.5 us -> 0 us
  between operations: 16.6 us -> 0.66 us
    psum x1 -> x0, waiting for transfers between devices: 212 us -> none  [shards(): lax.psum(as_sent(grouped), 'replica')]
    dot_general x99 -> x0, matrix products: 151 us -> none  [the longest x6 14.7 us: forward_parts(): gate_val = jnp.dot(second, w_gate, preferred_element_type=jnp.float32)]
    pallas_call x0 -> x2, Pallas kernels: none -> 113 us  [the longest x1 108 us: run_step(): pl.pallas_call(step_kernel, out_shape=[rows, rows, jax.ShapeDtypeStruct((...]
    psum x1 -> x0, blocking collectives: 82.1 us -> none  [shards(): lax.psum(as_sent(grouped), 'replica')]
    all_to_all x7 -> x0, starting transfers between devices: 27.9 us -> none  [summed_on_arrival(): lax.all_to_all(cut_along(shard, dim, length), axis, 0, 0, tiled=True)]
    convert_element_type x30 -> x0, other arithmetic: 19.4 us -> none  [the longest x7 9.23 us: shards(): part.astype(jnp.float32)]
    all_gather x2 -> x0, waiting for transfers between devices: 17.1 us -> none  [the longest x1 13.8 us: side_by_side(): result = lax.all_gather(both, axis, axis=dim, tiled=True)]
    ppermute x4 -> x0, starting transfers between devices: 15 us -> none  [passed_along(): return lax.ppermute(shard, axis, pairs)]
  transfers between devices with their start and end apart: 14 -> 0, of which waited for: 9 -> 0; matrix products, arithmetic and copies ran while one was open for 16% -> 0% of each run, Pallas kernels for 0% -> 0%
where the time goes in v2:
time: 114 us
  Pallas kernels  113 us (99%)
    pallas_call x1, Pallas kernels, run_step(): pl.pallas_call(step_kernel, out_shape=[rows, rows, jax.ShapeDtypeStruct((...  108 us
    pallas_call x1, Pallas kernels, run_unpack(): pl.pallas_call(unpack_kernel, out_shape=[jax.ShapeDtypeStruct(a.shape, a....  5.46 us

profile of v2, /device:TPU:0, one launch (start us, length us, event | category | flops | bytes accessed | tf_op | source)
XLA Modules:
  0.0 114.2 jit_solution(7628712960184443989)
XLA Ops:
  0.6 108.0 %shard_map.203 = (bf16[2,576,128]{2,1,0:T(8,128)(2,1)}, bf16[2,576,128]{2,1,0:T(8,128)(2,1)}, bf16[14336,128]{1,0:T(8,128)(2,1)}) custom-call(s32[2,2]{1,0:T(2,128)} %lens.1, bf16[2,576,128]{2,1,0:T(8,128)(2,1)} %bitcast.23, bf16[2,576,128]{2,1,0:T(8,128)(2,1)} %bitcast.24, bf16[1,288]{1,0:T(2,128)(2,1)} %gain_one.1, bf16[1,288]{1,0:T(2,128)(2,1)} %gain_two.1, ...), custom_call_target="tpu_custom_call" | custom-call | tf_op jit(solution)/shard_map/pallas_call | solution.py:730
  108.7 5.5 %shard_map.204 = (bf16[2,576,128]{2,1,0:T(8,128)(2,1)}, bf16[2,576,128]{2,1,0:T(8,128)(2,1)}, f32[1,288]{1,0:T(1,128)}, f32[1,288,576]{2,1,0:T(8,128)}, f32[1,28...) custom-call(bf16[14336,128]{1,0:T(8,128)(2,1)} %get-tuple-element.25, ...), custom_call_target="tpu_custom_call" | custom-call | tf_op jit(solution)/shard_map/pallas_call | solution.py:776

commit v3 on v2

v3 whole, which is shorter than its diff:
```python
import functools
import math
from types import SimpleNamespace

import jax
import jax.numpy as jnp
from jax import lax
from jax.experimental import pallas as pl
from jax.experimental.pallas import tpu as pltpu
from jax.sharding import PartitionSpec as P

MESH = pl.DeviceIdType.MESH
F32 = jnp.float32
BF16 = jnp.bfloat16

D = 576
HD = 64
FF = 1536
ROWS = 128
MICRO = 2
M = MICRO * ROWS
OWN = D // 2
EPS = 1e-05
BASE = 100000.0
VMEM_LIMIT = 62 * 1024 * 1024

GATE = 0
UP = GATE + 12 * OWN
DOWN = UP + 12 * OWN
QKV = DOWN + 6 * D
OUT = QKV + 8 * OWN
GAIN = OUT + 4 * OWN
USED = GAIN + OWN
FLAT = 14336
CHUNKS = (5120, 5120, 4096)
PARTS = 2 * len(CHUNKS)
SIZE = [n // 2 for n in CHUNKS for _ in range(2)]
BASE_ROW = [sum(SIZE[:i]) for i in range(PARTS)]


def dot(a, b):
    return lax.dot_general(a, b, (((1,), (0,)), ((), ())), preferred_element_type=F32)


def dot_nt(a, b):
    return lax.dot_general(a, b, (((1,), (1,)), ((), ())), preferred_element_type=F32)


def dot_tn(a, b):
    return lax.dot_general(a, b, (((0,), (0,)), ((), ())), preferred_element_type=F32)


def lanes():
    return lax.broadcasted_iota(jnp.int32, (ROWS, 128), 1)


def slots():
    return lax.broadcasted_iota(jnp.int32, (ROWS, 128), 0)


def segment_of(ids, first_end, last_end):
    return jnp.where(ids >= first_end, 1, 0) + jnp.where(ids >= last_end, 1, 0)


def turned(u, lane):
    return jnp.where(lane % 64 < 32, pltpu.roll(u, 96, 1), pltpu.roll(u, 32, 1))


def both_halves(u, half, lane):
    return jnp.where(lane // 64 == half, u, pltpu.roll(u, 64, 1))


def norm_scale(x):
    return lax.rsqrt(jnp.mean(x * x, axis=-1, keepdims=True) + EPS)


def norm_back(upper, normed, scale):
    return scale * (upper - normed * jnp.mean(upper * normed, axis=-1, keepdims=True))


def lengths_of(r, m):
    first = r.lens[m, 0:1, 0:1].astype(jnp.int32)
    return first, first + r.lens[m, 0:1, 1:2].astype(jnp.int32)


def tables(r, m):
    first_end, last_end = lengths_of(r, m)
    lane, slot = lanes(), slots()
    inverse = jnp.exp((lane % 32).astype(F32) * (-2.0 * math.log(BASE) / HD))
    position = slot - jnp.where(slot >= first_end, first_end, 0)
    position = position - jnp.where(slot >= last_end, last_end - first_end, 0)
    angle = position.astype(F32) * inverse
    sine = jnp.sin(angle)
    r.cs[m] = jnp.cos(angle)
    r.sn[m] = jnp.where(lane % 64 < 32, -sine, sine)


def side_rows(wq, wk, wv, gain_one, gain_two):
    lane = lax.broadcasted_iota(jnp.int32, (OWN, 128), 1)
    none = jnp.zeros((OWN, 64), F32)
    tail = jnp.concatenate([wq[:, 512:576].astype(F32), none], axis=1)
    key_a = pltpu.roll(wk[:, :128].astype(F32), 64, 1)
    key_b = pltpu.roll(jnp.concatenate([wk[:, 128:192].astype(F32), none], axis=1), 64, 1)
    last = jnp.concatenate([wv[:, 128:192].astype(F32), none], axis=1)
    row = lax.broadcasted_iota(jnp.int32, (128, OWN), 0)
    gains = jnp.where(
        row == 64, gain_one[...].astype(F32), jnp.where(row == 65, gain_two[...].astype(F32), 0.0)
    ).T
    return {
        512: jnp.where(lane < 64, tail, key_a),
        640: jnp.where(lane < 64, key_a, key_b),
        768: wv[:, :128].astype(F32),
        896: last + gains,
    }


def forward(r, m, arrived):
    x = r.x[m]
    n1 = x * norm_scale(x)
    wq, wo, wg, wu, wd = r.wq, r.wo, r.wg, r.wu, r.wd
    g1, g2 = r.gains[0:1, :], r.gains[1:2, :]
    entry = (n1 * g1).astype(BF16)
    r.ent[m] = entry
    qkv = dot(entry, wq[...])
    lane = lanes()
    cosine, sine = r.cs[m], r.sn[m]
    first_end, last_end = lengths_of(r, m)
    allowed = (
        segment_of(slots(), first_end, last_end) == segment_of(lane, first_end, last_end)
    ) & (lane <= slots())
    allowed = jnp.concatenate([allowed.astype(F32)] * 3, axis=0) > 0.5
    blocks = []
    for b in range(6):
        u = qkv[:, 128 * b : 128 * b + 128]
        blocks.append(u * cosine + turned(u, lane) * sine)
    groups = range(3)
    keys = [both_halves(blocks[(9 + g) // 2], (9 + g) % 2, lane).astype(BF16) for g in groups]
    values = [
        both_halves(qkv[:, 768 + 128 * (g // 2) : 896 + 128 * (g // 2)], g % 2, lane).astype(BF16)
        for g in groups
    ]
    queries = [
        jnp.concatenate(
            [
                jnp.where(lane // 64 == j % 2, blocks[j // 2], 0.0).astype(BF16)
                for j in range(3 * g, 3 * g + 3)
            ],
            axis=0,
        )
        for g in groups
    ]
    scores = [
        jnp.where(allowed, dot_nt(q, k) * HD**-0.5, -1e30) for q, k in zip(queries, keys)
    ]
    tops = [jnp.max(v, axis=-1, keepdims=True) for v in scores]
    weights = [jnp.exp(v - top) for v, top in zip(scores, tops)]
    sums = [jnp.sum(w, axis=-1, keepdims=True) for w in weights]
    probs = [w / total for w, total in zip(weights, sums)]
    outs = [dot(p.astype(BF16), v) for p, v in zip(probs, values)]
    heads = [out[ROWS * j : ROWS * (j + 1)] for out in outs for j in range(3)]
    for g in groups:
        r.kd[m, g] = keys[g]
        r.vd[m, g] = values[g]
        r.qs[m, g] = queries[g]
        r.pr[m, g] = probs[g]
    for b in range(4):
        r.mix[m, :, 128 * b : 128 * b + 128] = jnp.where(
            lane < 64, heads[2 * b], heads[2 * b + 1]
        ).astype(BF16)
    r.mix[m, :, 512:576] = heads[8][:, :64].astype(BF16)
    arrived("wo")
    middle = x + dot(r.mix[m], wo[...])
    r.mid[m] = middle
    second = (middle * norm_scale(middle) * g2).astype(BF16)
    r.sec[m] = second
    for j in range(0, FF, 256):
        cols = slice(j, j + 256)
        if j % (FF // 2) == 0:
            arrived("wg" + str(j))
            arrived("wu" + str(j))
        gate = dot(second, wg[:, cols])
        up = dot(second, wu[:, cols])
        sig = 1.0 / (1.0 + jnp.exp(-gate))
        swish = gate * sig
        r.inn[m, :, cols] = (swish * up).astype(BF16)
        r.fa[m, :, cols] = up * sig * (1.0 + gate * (1.0 - sig))
        r.fb[m, :, cols] = swish
    arrived("wd")
    return middle + dot_nt(r.inn[m], wd[...])


def backward(r, m, halfway):
    wq, wo, wg, wu, wd = r.wq, r.wo, r.wg, r.wu, r.wd
    g1, g2 = r.gains[0:1, :], r.gains[1:2, :]
    dy = r.dy[m]
    middle = r.mid[m]
    scale_two = norm_scale(middle)
    n2 = middle * scale_two
    df = dy.astype(BF16)
    r.df[m] = df
    for j in range(0, FF, 256):
        cols = slice(j, j + 256)
        d_inner = dot(df, wd[:, cols])
        r.dg[m, :, cols] = (d_inner * r.fa[m, :, cols]).astype(BF16)
        r.du[m, :, cols] = (d_inner * r.fb[m, :, cols]).astype(BF16)
    halfway()
    d_second = dot_nt(r.dg[m], wg[...]) + dot_nt(r.du[m], wu[...])
    r.gsum[m, 1:2, :] = jnp.sum(d_second * n2, axis=0, keepdims=True)
    d_middle = dy + norm_back(d_second * g2, n2, scale_two)
    branch = d_middle.astype(BF16)
    r.db[m] = branch
    d_mixed = dot_nt(branch, wo[...])
    lane = lanes()
    cosine, sine = r.cs[m], r.sn[m]
    groups = range(3)
    uppers = []
    for g in groups:
        parts = []
        for j in range(3 * g, 3 * g + 3):
            if j < 8:
                block = d_mixed[:, 128 * (j // 2) : 128 * (j // 2) + 128]
                block = jnp.where(lane // 64 == j % 2, block, 0.0)
            else:
                block = jnp.concatenate([d_mixed[:, 512:576], jnp.zeros((ROWS, 64), F32)], axis=1)
            parts.append(block.astype(BF16))
        uppers.append(jnp.concatenate(parts, axis=0))
    probs = [r.pr[m, g] for g in groups]
    d_probs = [dot_nt(uppers[g], r.vd[m, g]) for g in groups]
    dv = [dot_tn(probs[g].astype(BF16), uppers[g]) for g in groups]
    totals = [jnp.sum(d_probs[g] * probs[g], axis=-1, keepdims=True) for g in groups]
    d_scores = [
        (probs[g] * (d_probs[g] - totals[g]) * HD**-0.5).astype(BF16) for g in groups
    ]
    queries = [dot(d_scores[g], r.kd[m, g]) for g in groups]
    dk = [dot_tn(d_scores[g], r.qs[m, g]) for g in groups]
    dq = [q[ROWS * j : ROWS * (j + 1)] for q in queries for j in range(3)]
    dk = [key + pltpu.roll(key, 64, 1) for key in dk]
    dv = [value + pltpu.roll(value, 64, 1) for value in dv]
    heads = dq + dk
    for b in range(6):
        u = jnp.where(lane < 64, heads[2 * b], heads[2 * b + 1])
        r.dqkv[m, :, 128 * b : 128 * b + 128] = (u * cosine - turned(u, lane) * sine).astype(
            BF16
        )
    r.dqkv[m, :, 768:896] = jnp.where(lane < 64, dv[0], dv[1]).astype(BF16)
    r.dqkv[m, :, 896:1024] = jnp.where(lane < 64, dv[2], 0.0).astype(BF16)
    d_entry = dot_nt(r.dqkv[m], wq[...])
    x = r.x[m]
    scale_one = norm_scale(x)
    n1 = x * scale_one
    r.gsum[m, 0:1, :] = jnp.sum(d_entry * n1, axis=0, keepdims=True)
    return d_middle + norm_back(d_entry * g1, n1, scale_one)


def whole(ref, cols=slice(None)):
    value = ref[:, :, cols]
    return value.reshape(M, value.shape[-1])


def store(flat, start, block):
    flat[0, start : start + OWN] = block[:OWN].astype(BF16)
    flat[1, start : start + OWN] = block[OWN:].astype(BF16)


def gate_grads(r, flat, done):
    second_t = whole(r.sec).T
    for ref, start in ((r.dg, GATE), (r.du, UP)):
        for b in range(0, 12, 2):
            g = dot(second_t, whole(ref, slice(128 * b, 128 * b + 256)))
            store(flat, start + b * OWN, g[:, :128])
            store(flat, start + (b + 1) * OWN, g[:, 128:])
            done(start + (b + 2) * OWN)


def down_grads(r, flat, done):
    df_t = whole(r.df).T
    for b in range(6):
        for owner in range(2):
            first = 768 * owner + 128 * b
            g = dot(df_t, whole(r.inn, slice(first, first + 128)))
            flat[owner, DOWN + b * D : DOWN + (b + 1) * D] = g.astype(BF16)
        done(DOWN + (b + 1) * D)


def rest_grads(r, flat, done):
    entry_t = whole(r.ent).T
    mixed_t = whole(r.mix).T
    for b in range(0, 8, 2):
        g = dot(entry_t, whole(r.dqkv, slice(128 * b, 128 * b + 256)))
        store(flat, QKV + b * OWN, g[:, :128])
        if b == 6:
            rest = whole(r.db, slice(512, 576)).astype(F32)
            rest = jnp.concatenate([rest, jnp.zeros((M, 64), F32)], axis=1)
            rest = pltpu.roll(rest, 64, 1).astype(BF16)
            store(flat, QKV + 7 * OWN, g[:, 128:] + dot(mixed_t, rest))
        else:
            store(flat, QKV + (b + 1) * OWN, g[:, 128:])
        done(QKV + (b + 2) * OWN)
    for b in range(0, 4, 2):
        g = dot(mixed_t, whole(r.db, slice(128 * b, 128 * b + 256)))
        store(flat, OUT + b * OWN, g[:, :128])
        store(flat, OUT + (b + 1) * OWN, g[:, 128:])
        done(OUT + (b + 2) * OWN)
    sums = r.gsum[0] + r.gsum[1]
    row = lax.broadcasted_iota(jnp.int32, (128, D), 0)
    store(flat, GAIN, jnp.where(row == 0, sums[0:1], jnp.where(row == 1, sums[1:2], 0.0)).T)
    flat[0, USED:] = jnp.zeros((FLAT - USED, 128), BF16)
    flat[1, USED:] = jnp.zeros((FLAT - USED, 128), BF16)
    done(FLAT)


KEPT = dict(
    wq=((D, 1024), BF16),
    wo=((D, D), BF16),
    wg=((D, FF), BF16),
    wu=((D, FF), BF16),
    wd=((D, FF), BF16),
    gains=((8, D), F32),
    x=((MICRO, ROWS, D), F32),
    dy=((MICRO, ROWS, D), F32),
    lens=((MICRO, 8, 128), F32),
    lens_own=((MICRO, 8, 128), F32),
    lens_pair=((MICRO, 8, 128), F32),
    cot_pair=((MICRO, D, ROWS), BF16),
    y_send=((MICRO, ROWS, D), BF16),
    y_box=((MICRO, ROWS, D), BF16),
    y_turn=((MICRO, D, ROWS), BF16),
    dx_send=((MICRO, ROWS, D), BF16),
    dx_box=((MICRO, ROWS, D), BF16),
    dx_turn=((MICRO, D, ROWS), BF16),
    ent=((MICRO, ROWS, D), BF16),
    qs=((MICRO, 3, 3 * ROWS, 128), BF16),
    kd=((MICRO, 3, ROWS, 128), BF16),
    vd=((MICRO, 3, ROWS, 128), BF16),
    pr=((MICRO, 3, 3 * ROWS, 128), F32),
    mix=((MICRO, ROWS, D), BF16),
    mid=((MICRO, ROWS, D), F32),
    sec=((MICRO, ROWS, D), BF16),
    inn=((MICRO, ROWS, FF), BF16),
    fa=((MICRO, ROWS, FF), F32),
    fb=((MICRO, ROWS, FF), F32),
    cs=((MICRO, ROWS, 128), F32),
    sn=((MICRO, ROWS, 128), F32),
    df=((MICRO, ROWS, D), BF16),
    dg=((MICRO, ROWS, FF), BF16),
    du=((MICRO, ROWS, FF), BF16),
    db=((MICRO, ROWS, D), BF16),
    dqkv=((MICRO, ROWS, 1024), BF16),
    gsum=((MICRO, 8, D), F32),
    flat=((2, FLAT, 128), BF16),
    cross=((FLAT, 128), BF16),
    one=((6 * PARTS, max(SIZE) // 8, 128), BF16),
    two=((7 * PARTS, max(SIZE) // 32, 128), BF16),
    o=((FLAT, 128), BF16),
)
SEMS = dict(
    w=7,
    swap=2,
    y=2,
    dx=2,
    y_swap=2,
    dx_swap=2,
    cross=4 * PARTS,
    one=6 * PARTS,
    two=7 * PARTS,
    along=7 * PARTS,
    back=12 * PARTS,
)


def vmem(n):
    return [pl.BlockSpec(memory_space=pltpu.VMEM)] * n


def hbm(n):
    return [pl.BlockSpec(memory_space=pl.ANY)] * n


PLANE = [(0, 1), (1, 0), (3, 0), (1, 1), (3, 1), (2, 0), (2, 1)]


def places():
    section, core, replica = (lax.axis_index(a) for a in ("section", "shard", "replica"))
    x, y, z = replica // 8, replica // 2 % 4, replica % 2

    def at(x_, y_, z_):
        return (section, core, x_ * 8 + y_ * 2 + z_)

    return SimpleNamespace(
        section=section,
        core=core,
        x=x,
        y=y,
        z=z,
        x_next=at((x + 1) % 4, y, z),
        x_prev=at((x + 3) % 4, y, z),
        y_next=at(x, (y + 1) % 4, z),
        y_prev=at(x, (y + 3) % 4, z),
        z_pair=at(x, y, 1 - z),
        x_plane=[at((x + k) % 4, y, (z + w) % 2) for k, w in PLANE],
        y_plane=[at(x, (y + k) % 4, (z + w) % 2) for k, w in PLANE],
        partner=(section, 1 - core, replica),
        across=(1 - section, core, x * 8 + y * 2 + (1 - z)),
    )


def step_kernel(
    lens, tok, cot, gain_one, gain_two, wq_own, wk_own, wv_own, wo_own, wg_own, wu_own, wd_own,
    y_out, dx_out, o, *refs
):
    r = SimpleNamespace(**dict(zip(KEPT, refs)))
    sends = dict(zip(SEMS, refs[len(KEPT) :]))
    recvs = dict(zip(SEMS, refs[len(KEPT) + len(SEMS) :]))
    local = refs[len(KEPT) + 2 * len(SEMS)]
    at = places()
    section, core = at.section, at.core

    barrier = pltpu.get_barrier_semaphore()
    near = [at.partner, at.across, *at.x_plane, *at.y_plane[1:]]
    for device in near:
        pl.semaphore_signal(barrier, inc=1, device_id=device, device_id_type=MESH)
    def remote(name, i, src, dst, device):
        return pltpu.make_async_remote_copy(
            src,
            dst,
            sends[name].at[i],
            recvs[name].at[i],
            device_id=device,
            device_id_type=MESH,
        )

    own_rows = pl.ds(pl.multiple_of(core * OWN, 16), OWN)
    own_cols = pl.ds(pl.multiple_of(core * (FF // 2), 128), FF // 2)
    weight_places = {"wo": (wo_own, r.wo.at[own_rows])}
    for j in range(0, FF, FF // 2):
        cols = slice(j, j + FF // 2)
        weight_places["wg" + str(j)] = (wg_own.at[:, cols], r.wg.at[own_rows, cols])
        weight_places["wu" + str(j)] = (wu_own.at[:, cols], r.wu.at[own_rows, cols])
    weight_places["wd"] = (wd_own, r.wd.at[:, own_cols])
    side_place = r.wq.at[own_rows]
    weight_copies = {"side": [remote("w", 0, side_place, side_place, at.partner)]}
    for i, (name, (src, dst)) in enumerate(weight_places.items()):
        weight_copies[name] = [
            remote("w", i + 1, src, dst, at.partner),
            pltpu.make_async_copy(src, dst, local.at[i]),
        ]
        weight_copies[name][1].start()
    r.wq[own_rows, :512] = wq_own[:, :512]
    for start, value in side_rows(wq_own, wk_own, wv_own, gain_one, gain_two).items():
        r.wq[own_rows, start : start + 128] = value.astype(BF16)

    r.lens_own[...] = jnp.zeros((MICRO, 8, 128), F32)
    for m in range(MICRO):
        r.lens_own[m, 0:1, 0:2] = lens[m : m + 1, :].astype(F32)
    lens_swap = remote("swap", 0, r.lens_own, r.lens_pair, at.z_pair)
    cot_swap = remote("swap", 1, cot, r.cot_pair, at.z_pair)

    pl.semaphore_wait(barrier, len(near))
    for name in ("side", "wo"):
        weight_copies[name][0].start()
    lens_swap.start()
    cot_swap.start()

    @pl.when(section == 0)
    def _():
        r.lens[...] = r.lens_own[...]
        for m in range(MICRO):
            r.x[m] = tok[m].astype(F32).T

    @pl.when(section == 1)
    def _():
        lens_swap.wait_recv()
        r.lens[...] = r.lens_pair[...]

    for m in range(MICRO):
        tables(r, m)
    weight_copies["side"][0].wait_recv()
    for name in weight_places:
        if name != "wo":
            weight_copies[name][0].start()
    r.gains[...] = r.wq[:, 896:1024].astype(F32).T[64:72]

    def y_copy(m):
        return remote("y", m, r.y_send.at[m], r.y_box.at[m], at.across)

    def dx_copy(m):
        return remote("dx", m, r.dx_send.at[m], r.dx_box.at[m], at.across)

    def y_swap(m):
        return remote("y_swap", m, r.y_turn.at[m], y_out.at[m], at.z_pair)

    def dx_swap(m):
        return remote("dx_swap", m, r.dx_turn.at[m], dx_out.at[m], at.z_pair)

    total = Total(r, at, remote)

    def tick(t, carry):
        m = jnp.where(section == 0, t % 2, t // 2)
        ahead = jnp.where(section == 0, t // 2, t % 2) == 0

        @pl.when(ahead)
        def _():
            @pl.when(section == 1)
            def _():
                y_copy(m).wait_recv()
                r.x[m] = r.y_box[m].astype(F32)

            def arrived(name):
                @pl.when(t == 0)
                def _():
                    for i, copy in enumerate(weight_copies[name]):
                        if i == 0:
                            copy.wait_recv()
                        else:
                            copy.wait()

            y = forward(r, m, arrived)
            r.y_send[m] = y.astype(BF16)

            @pl.when(section == 0)
            def _():
                y_copy(m).start()
                y_out[m] = r.y_send[m].astype(F32).T.astype(BF16)

            @pl.when(section == 1)
            def _():
                r.y_turn[m] = r.y_send[m].astype(F32).T.astype(BF16)
                y_swap(m).start()

        @pl.when(jnp.logical_not(ahead))
        def _():
            @pl.when(section == 0)
            def _():
                dx_copy(m).wait_recv()
                r.dy[m] = r.dx_box[m].astype(F32)

            @pl.when(section == 1)
            def _():
                @pl.when(t == 1)
                def _():
                    cot_swap.wait_recv()

                ids = lax.broadcasted_iota(jnp.int32, (ROWS, D), 0)
                live = ids < lengths_of(r, m)[1]
                r.dy[m] = jnp.where(live, r.cot_pair[m].astype(F32).T, 0.0)

            def halfway():
                @pl.when(jnp.logical_and(section == 0, t == 2 * MICRO - 1))
                def _():
                    gate_grads(r, r.flat, total.starter())

            r.dx_send[m] = backward(r, m, halfway).astype(BF16)

            @pl.when(section == 0)
            def _():
                dx_out[m] = r.dx_send[m].astype(F32).T.astype(BF16)

            @pl.when(section == 1)
            def _():
                dx_copy(m).start()
                r.dx_turn[m] = r.dx_send[m].astype(F32).T.astype(BF16)
                dx_swap(m).start()

        return carry

    lax.fori_loop(0, 2 * MICRO, tick, 0)

    @pl.when(section == 0)
    def _():
        lens_swap.wait_recv()
        cot_swap.wait_recv()

    @pl.when(section == 1)
    def _():
        gate_grads(r, r.flat, total.starter())

    started = total.starter(DOWN)
    total.step_1(0)
    down_grads(r, r.flat, started)
    rest_grads(r, r.flat, started)
    total.run(o, local)
    total.finish()

    lens_swap.wait_send()
    cot_swap.wait_send()
    for copies in weight_copies.values():
        copies[0].wait_send()

    @pl.when(section == 0)
    def _():
        for m in range(MICRO):
            y_copy(m).wait_send()

    @pl.when(section == 1)
    def _():
        for m in range(MICRO):
            dx_copy(m).wait_send()
            y_swap(m).wait()
            dx_swap(m).wait()


def span(start, count):
    return pl.ds(pl.multiple_of(start, 16), count)


class Total:
    def __init__(self, r, at, remote):
        self.flat, self.box, self.one, self.two, self.o = r.flat, r.cross, r.one, r.two, r.o
        self.at, self.remote = at, remote
        self.core = at.core
        self.pos = ((at.x, at.y), (at.y, at.x))
        xs, ys = (at.x_next, at.x_prev), (at.y_next, at.y_prev)
        self.first = (xs, ys)
        self.plane = (at.y_plane, at.x_plane)
        self.sent = []
        self.copies = {}

    def send(self, name, i, src, dst, device):
        copy = self.remote(name, i, src, dst, device)
        copy.start()
        self.sent.append(copy)
        self.copies[name, i] = copy

    def got(self, name, i):
        self.copies[name, i].wait_recv()

    def cross(self, n):
        i, q = n // 4, n % 4
        count = SIZE[i] // 4
        rows = slice(BASE_ROW[i] + q * count, BASE_ROW[i] + (q + 1) * count)
        src = self.flat.at[1 - self.core, rows]
        return self.remote("cross", n, src, self.box.at[rows], self.at.partner)

    def starter(self, first=0):
        ends = [BASE_ROW[n // 4] + (n % 4 + 1) * SIZE[n // 4] // 4 for n in range(4 * PARTS)]
        begun = [sum(end <= first for end in ends)]

        def ready(rows):
            while begun[0] < len(ends) and ends[begun[0]] <= rows:
                self.cross(begun[0]).start()
                begun[0] += 1

        return ready

    def rows(self, i, k, start=0, count=None):
        place = SIZE[i] // 4 * ((self.pos[i % 2][0] + k) % 4)
        return span(BASE_ROW[i] + place + start, count)

    def piece(self, i, k):
        return SIZE[i] // 16 * ((self.pos[i % 2][1] + k) % 4)

    def add(self, i, k, upper, *others):
        count = SIZE[i] // 8
        rows = self.rows(i, k, upper * count, count)
        value = self.flat[self.core, rows].astype(F32) + self.box[rows].astype(F32)
        for other in others:
            value = value + other.astype(F32)
        self.flat[self.core, rows] = value.astype(BF16)
        return self.flat.at[self.core, rows]

    def go(self, i, slot, ref, way):
        device = self.first[i % 2][way]
        box = self.one.at[i * 6 + slot, : SIZE[i] // 8]
        self.send("one", i * 6 + slot, ref, box, device)

    def box_of(self, i, slot):
        self.got("one", i * 6 + slot)
        return self.one[i * 6 + slot, : SIZE[i] // 8]

    def step_1(self, c):
        for i in (2 * c, 2 * c + 1):
            for q in range(4):
                self.cross(i * 4 + q).wait_recv()
            self.go(i, 0, self.add(i, 2, 0), 0)
            self.go(i, 1, self.add(i, 2, 1), 1)
        for i in (2 * c, 2 * c + 1):
            self.go(i, 2, self.add(i, 1, 1), 0)
            self.go(i, 3, self.add(i, 3, 0), 1)

    def step_2(self, c):
        for i in (2 * c, 2 * c + 1):
            self.go(i, 4, self.add(i, 1, 0, self.box_of(i, 0)), 0)
            self.go(i, 5, self.add(i, 3, 1, self.box_of(i, 1)), 1)

    def block(self, i, k, w):
        count = SIZE[i] // 32
        return self.rows(i, 0, self.piece(i, k) + count * ((self.at.z + w) % 2), count)

    def two_box(self, i, j):
        return self.two.at[i * 7 + j, : SIZE[i] // 32]

    def step_3(self, c):
        for i in (2 * c, 2 * c + 1):
            self.add(i, 0, 0, self.box_of(i, 3), self.box_of(i, 4))
            self.add(i, 0, 1, self.box_of(i, 2), self.box_of(i, 5))
            for j, (k, w) in enumerate(PLANE):
                src = self.flat.at[self.core, self.block(i, k, w)]
                self.send("two", i * 7 + j, src, self.two_box(i, j), self.plane[i % 2][j])

    def step_4(self, c):
        for i in (2 * c, 2 * c + 1):
            rows = self.block(i, 0, 0)
            value = self.flat[self.core, rows].astype(F32)
            for j in range(7):
                self.got("two", i * 7 + j)
                value = value + self.two[i * 7 + j, : SIZE[i] // 32].astype(F32)
            self.o[rows] = value.astype(BF16)
            ref = self.o.at[rows]
            for j in range(7):
                self.send("along", i * 7 + j, ref, ref, self.plane[i % 2][j])

    def unit(self, i, k1, k2):
        return self.o.at[self.rows(i, k1, self.piece(i, k2), SIZE[i] // 16)]

    def step_5(self, c):
        for k in (0, 1, 3, 2):
            for i in (2 * c, 2 * c + 1):
                for j, (there, _) in enumerate(PLANE):
                    if there == k:
                        self.got("along", i * 7 + j)
                back = (4 - k) % 4
                ref = self.unit(i, 0, back)
                for d in range(2):
                    self.send("back", i * 12 + d * 6 + back, ref, ref, self.first[i % 2][d])

    def step_6(self, c):
        for k in (0, 3, 1, 2):
            for i in (2 * c, 2 * c + 1):
                self.got("back", i * 12 + k)
                self.got("back", i * 12 + 6 + k)
                way = 0 if k in (0, 3) else 1
                ref = self.unit(i, 1 if way else 3, k)
                slot = i * 12 + way * 6 + (4 if k < 2 else 5)
                self.send("back", slot, ref, ref, self.first[i % 2][way])

    def step_7(self, c):
        for i in (2 * c, 2 * c + 1):
            for slot in (4, 5, 10, 11):
                self.got("back", i * 12 + slot)
        rows = slice(BASE_ROW[2 * c], BASE_ROW[2 * c] + CHUNKS[c])
        copy = pltpu.make_async_copy(self.o.at[rows], self.out.at[rows], self.sem.at[c])
        copy.start()
        self.written.append(copy)

    def run(self, out, sem):
        self.out, self.sem, self.written = out, sem, []
        for n in range(2, 7 + len(CHUNKS)):
            for c in range(len(CHUNKS)):
                if 1 <= n - c <= 7:
                    getattr(self, f"step_{n - c}")(c)
        for copy in self.written:
            copy.wait()

    def finish(self):
        for n in range(4 * PARTS):
            self.cross(n).wait_send()
        for copy in self.sent:
            copy.wait_send()


def run_step(lens, tok, cot, gain_one, gain_two, wq, wk, wv, wo, wg, wu, wd):
    rows = jax.ShapeDtypeStruct((MICRO, D, ROWS), BF16)
    sems = [pltpu.SemaphoreType.DMA((n,)) for n in SEMS.values()]
    return pl.pallas_call(
        step_kernel,
        out_shape=[rows, rows, jax.ShapeDtypeStruct((FLAT, 128), BF16)],
        in_specs=vmem(8) + hbm(4),
        out_specs=vmem(2) + hbm(1),
        scratch_shapes=[pltpu.VMEM(*v) for v in KEPT.values()]
        + sems
        + sems
        + [pltpu.SemaphoreType.DMA((6,))],
        compiler_params=pltpu.CompilerParams(
            collective_id=1, has_side_effects=True, vmem_limit_bytes=VMEM_LIMIT
        ),
    )(lens, tok, cot, gain_one, gain_two, wq, wk, wv, wo, wg, wu, wd)


def unpack_kernel(
    f, y, dx, y_out, dx_out, gain_one, wq, wk, wv, wo, gain_two, wg, wu, wd, *refs
):
    flat, s_y, s_dx, s_wq, s_wk, s_wv, s_wo, s_wg, s_wu, s_wd, arrive, leave = refs
    step = 6 * OWN
    bounds = (*range(0, QKV, step), QKV, USED)
    loads = []

    def load(src, dst):
        loads.append(pltpu.make_async_copy(src, dst, arrive.at[len(loads)]))
        loads[-1].start()

    for i in range(len(bounds) - 1):
        part = slice(bounds[i], bounds[i + 1])
        load(f.at[part], flat.at[part])
    load(y, s_y)
    load(dx, s_dx)
    stores = []

    def put(src, dst):
        stores.append(pltpu.make_async_copy(src, dst, leave.at[len(stores)]))
        stores[-1].start()

    def rows(start, count=OWN):
        return flat[start : start + count].astype(F32)

    n = 0
    for start, stage, dst in ((GATE, s_wg, wg), (UP, s_wu, wu)):
        for j in range(0, 12, 6):
            loads[n].wait()
            n += 1
            for b in range(j, j + 6):
                stage[:, 128 * b : 128 * b + 128] = rows(start + b * OWN)
            cols = slice(128 * j, 128 * j + 768)
            put(stage.at[:, cols], dst.at[0, :, cols])
    for j in range(0, 6, 3):
        loads[n].wait()
        n += 1
        for b in range(j, j + 3):
            s_wd[:, 128 * b : 128 * b + 128] = rows(DOWN + b * D, D)
        cols = slice(128 * j, 128 * j + 384)
        put(s_wd.at[:, cols], wd.at[0, :, cols])
    loads[n].wait()
    n += 1
    swap = [pltpu.roll(rows(QKV + b * OWN), 64, 1) for b in range(4, 8)]
    lane = lax.broadcasted_iota(jnp.int32, (OWN, 128), 1)
    for b in range(4):
        s_wq[:, 128 * b : 128 * b + 128] = rows(QKV + b * OWN)
        s_wo[:, 128 * b : 128 * b + 128] = rows(OUT + b * OWN)
    s_wq[:, 512:576] = rows(QKV + 4 * OWN)[:, :64]
    put(s_wq, wq.at[0])
    s_wo[:, 512:576] = swap[3][:, :64]
    put(s_wo, wo.at[0])
    s_wk[:, :128] = jnp.where(lane < 64, swap[0], swap[1])
    s_wk[:, 128:] = swap[1][:, :64]
    put(s_wk, wk.at[0])
    s_wv[:, :128] = rows(QKV + 6 * OWN)
    s_wv[:, 128:] = rows(QKV + 7 * OWN)[:, :64]
    put(s_wv, wv.at[0])
    for src, dst in ((s_y, y_out), (s_dx, dx_out)):
        loads[n].wait()
        n += 1
        put(src, dst)
    gains = rows(GAIN).T
    gain_one[...] = gains[0:1]
    gain_two[...] = gains[1:2]
    for copy in stores:
        copy.wait()


def run_unpack(flat, y, dx):
    kinds = [(1, OWN), (1, OWN, D), (1, OWN, 192), (1, OWN, 192), (1, OWN, D)]
    kinds += [(1, OWN), (1, OWN, FF), (1, OWN, FF), (1, D, FF // 2)]
    stages = [pltpu.VMEM(k[1:], F32) for k in kinds if len(k) == 3]
    return pl.pallas_call(
        unpack_kernel,
        out_shape=[jax.ShapeDtypeStruct(a.shape, a.dtype) for a in (y, dx)]
        + [jax.ShapeDtypeStruct(k, F32) for k in kinds],
        in_specs=hbm(3),
        out_specs=hbm(2) + [(vmem if len(k) == 2 else hbm)(1)[0] for k in kinds],
        scratch_shapes=[pltpu.VMEM((FLAT, 128), BF16)]
        + [pltpu.VMEM(y.shape, y.dtype)] * 2
        + stages
        + [pltpu.SemaphoreType.DMA((9,)), pltpu.SemaphoreType.DMA((12,))],
        compiler_params=pltpu.CompilerParams(vmem_limit_bytes=VMEM_LIMIT),
    )(flat, y, dx)


def shards(
    tokens,
    cotangent,
    seq_lengths,
    gain_attn,
    w_query,
    w_key,
    w_value,
    w_out,
    gain_ffn,
    w_gate,
    w_up,
    w_down,
):
    y, dx, flat = run_step(
        seq_lengths,
        jnp.swapaxes(tokens, 1, 2),
        jnp.swapaxes(cotangent, 1, 2),
        gain_attn,
        gain_ffn,
        w_query[0],
        w_key[0],
        w_value[0],
        w_out[0],
        w_gate[0],
        w_up[0],
        w_down[0].T,
    )
    y, dx, *grads = run_unpack(flat, y, dx)
    grads[8] = jnp.swapaxes(grads[8], 1, 2)
    return (jnp.swapaxes(y, 1, 2)[None], jnp.swapaxes(dx, 1, 2)[None], *grads)


def solution(mesh):
    row_spec = P(None, ("shard", "replica"), None)
    out_spec = P("section", None, ("shard", "replica"), None)
    vector = P("section", "shard")
    matrix = P("section", "shard", None)
    weight_specs = (vector, matrix, matrix, matrix, matrix, vector, matrix, matrix, matrix)
    return jax.shard_map(
        shards,
        mesh=mesh,
        in_specs=(row_spec, row_spec, P(None, ("shard", "replica")), *weight_specs),
        out_specs=(out_spec, out_spec, *weight_specs),
        check_vma=False,
    )
```

time: 114 us -> 105 us (0.921)
  Pallas kernels: 113 us -> 104 us
    pallas_call x1, Pallas kernels: 108 us -> 99.4 us  [run_step(): pl.pallas_call(step_kernel, out_shape=[rows, rows, jax.ShapeDtypeStruct((...]
where the time goes in v3:
time: 105 us
  Pallas kernels  104 us (99%)
    pallas_call x1, Pallas kernels, run_step(): pl.pallas_call(step_kernel, out_shape=[rows, rows, jax.ShapeDtypeStruct((...  99.4 us
    pallas_call x1, Pallas kernels, run_unpack(): pl.pallas_call(unpack_kernel, out_shape=[jax.ShapeDtypeStruct(a.shape, a....  5.01 us

profile of v3, /device:TPU:0, one launch (start us, length us, event | category | flops | bytes accessed | tf_op | source)
XLA Modules:
  0.0 105.2 jit_solution(211935217187159270)
XLA Ops:
  0.6 99.4 %shard_map.203 = (bf16[2,576,128]{2,1,0:T(8,128)(2,1)}, bf16[2,576,128]{2,1,0:T(8,128)(2,1)}, bf16[14336,128]{1,0:T(8,128)(2,1)}) custom-call(s32[2,2]{1,0:T(2,128)} %lens.1, bf16[2,576,128]{2,1,0:T(8,128)(2,1)} %bitcast.23, bf16[2,576,128]{2,1,0:T(8,128)(2,1)} %bitcast.24, bf16[1,288]{1,0:T(2,128)(2,1)} %gain_one.1, bf16[1,288]{1,0:T(2,128)(2,1)} %gain_two.1, ...), custom_call_target="tpu_custom_call" | custom-call | tf_op jit(solution)/shard_map/pallas_call | solution.py:764
  100.1 5.0 %shard_map.204 = (bf16[2,576,128]{2,1,0:T(8,128)(2,1)}, bf16[2,576,128]{2,1,0:T(8,128)(2,1)}, f32[1,288]{1,0:T(1,128)}, f32[1,288,576]{2,1,0:T(8,128)}, f32[1,28...) custom-call(bf16[14336,128]{1,0:T(8,128)(2,1)} %get-tuple-element.25, ...), custom_call_target="tpu_custom_call" | custom-call | tf_op jit(solution)/shard_map/pallas_call | solution.py:853

commit v4 on v3

--- a/solution.py
+++ b/solution.py
@@ -322,6 +322,7 @@
     lens_own=((MICRO, 8, 128), F32),
     lens_pair=((MICRO, 8, 128), F32),
     cot_pair=((MICRO, D, ROWS), BF16),
+    tok=((MICRO, D, ROWS), BF16),
     y_send=((MICRO, ROWS, D), BF16),
     y_box=((MICRO, ROWS, D), BF16),
     y_turn=((MICRO, D, ROWS), BF16),
@@ -429,6 +430,12 @@
             device_id_type=MESH,
         )
 
+    tok_load = pltpu.make_async_copy(tok, r.tok, local.at[6])
+
+    @pl.when(section == 0)
+    def _():
+        tok_load.start()
+
     own_rows = pl.ds(pl.multiple_of(core * OWN, 16), OWN)
     own_cols = pl.ds(pl.multiple_of(core * (FF // 2), 128), FF // 2)
     weight_places = {"wo": (wo_own, r.wo.at[own_rows])}
@@ -464,8 +471,9 @@
     @pl.when(section == 0)
     def _():
         r.lens[...] = r.lens_own[...]
+        tok_load.wait()
         for m in range(MICRO):
-            r.x[m] = tok[m].astype(F32).T
+            r.x[m] = r.tok[m].astype(F32).T
 
     @pl.when(section == 1)
     def _():
@@ -488,6 +496,12 @@
 
     def y_swap(m):
         return remote("y_swap", m, r.y_turn.at[m], y_out.at[m], at.z_pair)
+
+    def y_store(m):
+        return pltpu.make_async_copy(r.y_turn.at[m], y_out.at[m], local.at[6 + m])
+
+    def dx_store(m):
+        return pltpu.make_async_copy(r.dx_turn.at[m], dx_out.at[m], local.at[8 + m])
 
     def dx_swap(m):
         return remote("dx_swap", m, r.dx_turn.at[m], dx_out.at[m], at.z_pair)
@@ -520,7 +534,8 @@
             @pl.when(section == 0)
             def _():
                 y_copy(m).start()
-                y_out[m] = r.y_send[m].astype(F32).T.astype(BF16)
+                r.y_turn[m] = r.y_send[m].astype(F32).T.astype(BF16)
+                y_store(m).start()
 
             @pl.when(section == 1)
             def _():
@@ -553,7 +568,8 @@
 
             @pl.when(section == 0)
             def _():
-                dx_out[m] = r.dx_send[m].astype(F32).T.astype(BF16)
+                r.dx_turn[m] = r.dx_send[m].astype(F32).T.astype(BF16)
+                dx_store(m).start()
 
             @pl.when(section == 1)
             def _():
@@ -590,6 +606,8 @@
     def _():
         for m in range(MICRO):
             y_copy(m).wait_send()
+            y_store(m).wait()
+            dx_store(m).wait()
 
     @pl.when(section == 1)
     def _():
@@ -764,12 +782,12 @@
     return pl.pallas_call(
         step_kernel,
         out_shape=[rows, rows, jax.ShapeDtypeStruct((FLAT, 128), BF16)],
-        in_specs=vmem(8) + hbm(4),
-        out_specs=vmem(2) + hbm(1),
+        in_specs=vmem(1) + hbm(2) + vmem(5) + hbm(4),
+        out_specs=hbm(3),
         scratch_shapes=[pltpu.VMEM(*v) for v in KEPT.values()]
         + sems
         + sems
-        + [pltpu.SemaphoreType.DMA((6,))],
+        + [pltpu.SemaphoreType.DMA((10,))],
         compiler_params=pltpu.CompilerParams(
             collective_id=1, has_side_effects=True, vmem_limit_bytes=VMEM_LIMIT
         ),

time: 105 us -> 104 us (level)
  no operation moved by 1% of the time
where the time goes in v4:
time: 104 us
  Pallas kernels  103 us (99%)
    pallas_call x1, Pallas kernels, run_step(): pl.pallas_call(step_kernel, out_shape=[rows, rows, jax.ShapeDtypeStruct((...  98.5 us
    pallas_call x1, Pallas kernels, run_unpack(): pl.pallas_call(unpack_kernel, out_shape=[jax.ShapeDtypeStruct(a.shape, a....  5.01 us

profile of v4, /device:TPU:0, one launch (start us, length us, event | category | flops | bytes accessed | tf_op | source)
XLA Modules:
  0.0 104.3 jit_solution(12336578007448600819)
XLA Ops:
  0.6 98.5 %shard_map.203 = (bf16[2,576,128]{2,1,0:T(8,128)(2,1)}, bf16[2,576,128]{2,1,0:T(8,128)(2,1)}, bf16[14336,128]{1,0:T(8,128)(2,1)}) custom-call(s32[2,2]{1,0:T(2,128)} %lens.1, bf16[2,576,128]{2,1,0:T(8,128)(2,1)} %bitcast.23, bf16[2,576,128]{2,1,0:T(8,128)(2,1)} %bitcast.24, bf16[1,288]{1,0:T(2,128)(2,1)} %gain_one.1, bf16[1,288]{1,0:T(2,128)(2,1)} %gain_two.1, ...), custom_call_target="tpu_custom_call" | custom-call | tf_op jit(solution)/shard_map/pallas_call | solution.py:782
  99.1 5.0 %shard_map.204 = (bf16[2,576,128]{2,1,0:T(8,128)(2,1)}, bf16[2,576,128]{2,1,0:T(8,128)(2,1)}, f32[1,288]{1,0:T(1,128)}, f32[1,288,576]{2,1,0:T(8,128)}, f32[1,28...) custom-call(bf16[14336,128]{1,0:T(8,128)(2,1)} %get-tuple-element.25, ...), custom_call_target="tpu_custom_call" | custom-call | tf_op jit(solution)/shard_map/pallas_call | solution.py:871

commit v5 on v4

--- a/solution.py
+++ b/solution.py
@@ -744,16 +744,15 @@
     def step_6(self, c):
         for k in (0, 3, 1, 2):
             for i in (2 * c, 2 * c + 1):
-                self.got("back", i * 12 + k)
-                self.got("back", i * 12 + 6 + k)
                 way = 0 if k in (0, 3) else 1
+                self.got("back", i * 12 + way * 6 + k)
                 ref = self.unit(i, 1 if way else 3, k)
                 slot = i * 12 + way * 6 + (4 if k < 2 else 5)
                 self.send("back", slot, ref, ref, self.first[i % 2][way])
 
     def step_7(self, c):
         for i in (2 * c, 2 * c + 1):
-            for slot in (4, 5, 10, 11):
+            for slot in (1, 2, 6, 9, 4, 5, 10, 11):
                 self.got("back", i * 12 + slot)
         rows = slice(BASE_ROW[2 * c], BASE_ROW[2 * c] + CHUNKS[c])
         copy = pltpu.make_async_copy(self.o.at[rows], self.out.at[rows], self.sem.at[c])

time: 104 us -> 104 us (level)
  no operation moved by 1% of the time
where the time goes in v5:
time: 104 us; the launch traced here: 103 us
  Pallas kernels  103 us (99%)
    pallas_call x1, Pallas kernels, run_step(): pl.pallas_call(step_kernel, out_shape=[rows, rows, jax.ShapeDtypeStruct((...  97.6 us
    pallas_call x1, Pallas kernels, run_unpack(): pl.pallas_call(unpack_kernel, out_shape=[jax.ShapeDtypeStruct(a.shape, a....  5.01 us

profile of v5, /device:TPU:0, one launch (start us, length us, event | category | flops | bytes accessed | tf_op | source)
XLA Modules:
  0.0 103.4 jit_solution(15763912034554844529)
XLA Ops:
  0.6 97.6 %shard_map.203 = (bf16[2,576,128]{2,1,0:T(8,128)(2,1)}, bf16[2,576,128]{2,1,0:T(8,128)(2,1)}, bf16[14336,128]{1,0:T(8,128)(2,1)}) custom-call(s32[2,2]{1,0:T(2,128)} %lens.1, bf16[2,576,128]{2,1,0:T(8,128)(2,1)} %bitcast.23, bf16[2,576,128]{2,1,0:T(8,128)(2,1)} %bitcast.24, bf16[1,288]{1,0:T(2,128)(2,1)} %gain_one.1, bf16[1,288]{1,0:T(2,128)(2,1)} %gain_two.1, ...), custom_call_target="tpu_custom_call" | custom-call | tf_op jit(solution)/shard_map/pallas_call | solution.py:781
  98.2 5.0 %shard_map.204 = (bf16[2,576,128]{2,1,0:T(8,128)(2,1)}, bf16[2,576,128]{2,1,0:T(8,128)(2,1)}, f32[1,288]{1,0:T(1,128)}, f32[1,288,576]{2,1,0:T(8,128)}, f32[1,28...) custom-call(bf16[14336,128]{1,0:T(8,128)(2,1)} %get-tuple-element.25, ...), custom_call_target="tpu_custom_call" | custom-call | tf_op jit(solution)/shard_map/pallas_call | solution.py:870
